TPU v7x, 32 devices: a whole 2x2x4 slice. The times are simulated.
32 devices in a mesh: batch: 2 (over x), blk: 4 (over z), uly: 4 (over y, core).
Axes of the slice: x: 2, y: 2, z: 4, core: 2. Of those that a mesh axis runs over, the one named last changes fastest.
Arguments:
- tokens: bfloat16 [2, 2048, 2048], P('batch', ('blk', 'uly')), may hold values from -6 to 6
- segments: int32 [2, 2048], P('batch'), may hold values from 0 to 18, as said below
- routes: int32 [2, 2048, 8], P('batch', ('blk', 'uly')), may hold values from 0 to 15, all different within a row; in each aligned block of 128 rows (0 to 127, 128 to 255, ..., all dimensions but the last counted through in order) at most 96 rows name the same one
- w_qkv: bfloat16 [2048, 6144], P(('batch', 'blk', 'uly')), may hold values from -0.125 to 0.125
- w_out: bfloat16 [2048, 2048], P(('batch', 'blk', 'uly')), may hold values from -4 to 4
- attn_gain: bfloat16 [2048], P(('batch', 'blk', 'uly')), may hold values from 0.5 to 1.5
- ffn_gain: bfloat16 [2048], P(('batch', 'blk', 'uly')), may hold values from 0.5 to 1.5
- qk_gain: bfloat16 [2, 128], replicated, may hold values from 1 to 2
- router: bfloat16 [2048, 16], P(('batch', 'blk', 'uly')), may hold values from -0.0625 to 0.0625
- w_gate_up: bfloat16 [16, 2048, 2048], P('blk', ('batch', 'uly')), may hold values from -0.125 to 0.125
- w_down: bfloat16 [16, 2048, 1024], P('blk', ('batch', 'uly')), may hold values from -1.5 to 1.5
- cotangent: bfloat16 [2, 2048, 2048], P('batch', ('blk', 'uly')), may hold values from -6 to 6
Outputs:
- output: bfloat16 [2, 2048, 2048], P('batch', ('blk', 'uly'))
- grad_tokens: float32 [2, 2048, 2048], P('batch', ('blk', 'uly'))
- grad_qkv: float32 [2048, 6144], P(('batch', 'blk', 'uly'))
- grad_out: float32 [2048, 2048], P(('batch', 'blk', 'uly'))
- grad_attn_gain: float32 [2048], P(('batch', 'blk', 'uly'))
- grad_ffn_gain: float32 [2048], P(('batch', 'blk', 'uly'))
- grad_qk_gain: float32 [2, 128], replicated
- grad_router: float32 [2048, 16], P(('batch', 'blk', 'uly'))
- grad_gate_up: float32 [16, 2048, 2048], P('blk', ('batch', 'uly'))
- grad_down: float32 [16, 2048, 1024], P('blk', ('batch', 'uly'))
- clipped_qkv: float32 [2048, 6144], P(('batch', 'blk', 'uly'))
Inputs may be any that keep to these rules, and one draw needn't show every extreme that they name: `routes`: within the tokens of one device (aligned blocks of 128 tokens) no expert is named more than 96 times, a bound that some block reaches; a token names 8 different experts. `segments`: numbers never fall along a sequence; equal numbers mark one document.
All inputs are finite; a program needn't handle non-finite values.
Results may differ from a plain program's by a relative error of at most 0.025.
Values may be sent and summed in bfloat16 or wider, within the bound.
A program may use at most 384 MiB of HBM per device.

v0:
```python
import functools
import math

import jax
import jax.numpy as jnp
from jax import lax
from jax.experimental import pallas as pl
from jax.experimental.pallas import tpu as pltpu
from jax.sharding import Mesh
from jax.sharding import PartitionSpec as P

EPS = 1e-06
THETA = 50000.0
TAU = 4.0
NEG = -1e30
LOG2E = 1.4426950408889634
LANES = 128
MOST_TOKENS = 512
VMEM_LIMIT = 60 * 1024 * 1024

ULY = ("y", "core")
ALL = ("batch", "blk", *ULY)
ROWS = ("batch", "blk")
PLANE = ("batch", *ULY)
CHIPS = ("batch", "y")

MESH = pl.DeviceIdType.MESH
BF16 = jnp.bfloat16
F32 = jnp.float32


def rms_scale(values):
    return lax.rsqrt(jnp.mean(values * values, axis=-1, keepdims=True) + EPS)


def norm_back(grad_normed, values, scale):
    normed = values * scale
    return scale * (grad_normed - normed * jnp.mean(grad_normed * normed, axis=-1, keepdims=True))


def rope_tables(offset, length, head_dim):
    half_dim = head_dim // 2
    frequency = THETA ** (-jnp.arange(half_dim, dtype=F32) * 2.0 / head_dim)
    positions = (offset + jnp.arange(length, dtype=jnp.int32)).astype(F32)
    angles = positions[:, None] * frequency[None, :]
    return (jnp.cos(angles)[:, None, :], jnp.sin(angles)[:, None, :])


def rope_rows(length, head_dim):
    fine = math.gcd(length, LANES)
    frequency = THETA ** (-jnp.arange(head_dim // 2, dtype=F32) * 2.0 / head_dim)
    frequency = jnp.concatenate([frequency, frequency])
    coarse_angle = (jnp.arange(length // fine, dtype=F32) * fine)[:, None, None] * frequency
    fine_angle = jnp.arange(fine, dtype=F32)[None, :, None] * frequency
    cos_a, sin_a, cos_b, sin_b = lax.optimization_barrier(
        (jnp.cos(coarse_angle), jnp.sin(coarse_angle), jnp.cos(fine_angle), jnp.sin(fine_angle))
    )
    sign = jnp.where(jnp.arange(head_dim) < head_dim // 2, -1.0, 1.0)
    cos = cos_a * cos_b - sin_a * sin_b
    sin = (sin_a * cos_b + cos_a * sin_b) * sign
    return cos.reshape(length, head_dim), sin.reshape(length, head_dim)


def rotate(values, cos_table, sin_table):
    half_dim = values.shape[-1] // 2
    first = values[..., :half_dim]
    second = values[..., half_dim:]
    return jnp.concatenate(
        [first * cos_table - second * sin_table, second * cos_table + first * sin_table], axis=-1
    )


def dot_nn(a, b):
    return lax.dot_general(a, b, (((1,), (0,)), ((), ())), preferred_element_type=F32)


def dot_nt(a, b):
    return lax.dot_general(a, b, (((1,), (1,)), ((), ())), preferred_element_type=F32)


def dot_tn(a, b):
    return lax.dot_general(a, b, (((0,), (0,)), ((), ())), preferred_element_type=F32)


def key_chunks(length):
    size = min(512, length)
    return size, length // size


def attn_fwd_kernel(factor, q_ref, k_ref, v_ref, sq_ref, sk_ref, o_ref, of_ref, lse_ref, top_ref, vt_ref):
    length = k_ref.shape[1]
    size, count = key_chunks(length)
    tile, head_dim = q_ref.shape[1:]

    @pl.when(pl.program_id(1) == 0)
    def _():
        vt_ref[...] = v_ref[0].astype(F32).T.astype(BF16)

    q = q_ref[0]
    seg_q = sq_ref[...]

    def step(j, carried):
        total, top, acc = carried
        at = pl.multiple_of(j * size, size)
        scores = dot_nt(k_ref[0, pl.ds(at, size), :], q)
        scores = jnp.where(sk_ref[pl.ds(at, size), :] == seg_q, scores, NEG)
        top = jnp.maximum(top, jnp.max(scores, axis=0, keepdims=True))
        weights = jnp.exp2(scores * factor)
        total = total + jnp.sum(weights, axis=0, keepdims=True)
        acc = acc + dot_nn(vt_ref[:, pl.ds(at, size)], weights.astype(BF16))
        return total, top, acc

    start = (
        jnp.zeros((1, tile), F32),
        jnp.full((1, tile), NEG, F32),
        jnp.zeros((head_dim, tile), F32),
    )
    total, top, acc = lax.fori_loop(0, count, step, start, unroll=count <= 4)
    out = (acc * (1.0 / total)).T
    o_ref[0] = out.astype(BF16)
    of_ref[0] = out
    lse_ref[0] = jnp.log2(total)
    top_ref[0] = top


def attn_bwd_kernel(
    factor, scale, q_ref, k_ref, v_ref, do_ref, of_ref, lse_ref, sq_ref, sk_ref,
    dq_ref, dk_ref, dv_ref, kt_ref, dk_acc, dv_acc,
):
    length = k_ref.shape[1]
    size, count = key_chunks(length)
    tile, head_dim = q_ref.shape[1:]

    @pl.when(pl.program_id(1) == 0)
    def _():
        kt_ref[...] = k_ref[0].astype(F32).T.astype(BF16)
        dk_acc[...] = jnp.zeros_like(dk_acc)
        dv_acc[...] = jnp.zeros_like(dv_acc)

    q = q_ref[0]
    grad = do_ref[0]
    seg_q = sq_ref[...]
    lse = lse_ref[0]
    row_dot = jnp.sum((grad.astype(F32) * of_ref[0]).T, axis=0, keepdims=True)

    def step(j, dq_t):
        at = pl.multiple_of(j * size, size)
        rows = pl.ds(at, size)
        scores = dot_nt(k_ref[0, rows, :], q)
        scores = jnp.where(sk_ref[rows, :] == seg_q, scores, NEG)
        weights = jnp.exp2(scores * factor - lse)
        grad_weights = dot_nt(v_ref[0, rows, :], grad)
        grad_scores = (weights * (grad_weights - row_dot)).astype(BF16)
        dk_acc[rows, :] += dot_nn(grad_scores, q)
        dv_acc[rows, :] += dot_nn(weights.astype(BF16), grad)
        return dq_t + dot_nn(kt_ref[:, rows], grad_scores)

    dq_t = lax.fori_loop(0, count, step, jnp.zeros((head_dim, tile), F32), unroll=count <= 4)
    dq_ref[0] = (dq_t * scale).T.astype(BF16)

    @pl.when(pl.program_id(1) == pl.num_programs(1) - 1)
    def _():
        dk_ref[0] = (dk_acc[...] * scale).astype(BF16)
        dv_ref[0] = dv_acc[...].astype(BF16)


def attention_tile(queries, length):
    return min(queries, 256 if length <= 4096 else 128)


def attention_forward(q_src, kv_src, cols, seg_q, seg_k, head_dim):
    heads, queries = q_src.shape[:2]
    length = kv_src.shape[1]
    tile = attention_tile(queries, length)
    q_col, k_col, v_col = cols
    factor = head_dim**-0.5 * LOG2E
    row = pl.BlockSpec((1, 1, tile), lambda h, i: (h, 0, i))
    block = pl.BlockSpec((1, tile, head_dim), lambda h, i: (h, i, 0))
    return pl.pallas_call(
        functools.partial(attn_fwd_kernel, factor),
        grid=(heads, queries // tile),
        in_specs=[
            pl.BlockSpec((1, tile, head_dim), lambda h, i: (h, i, q_col)),
            pl.BlockSpec((1, length, head_dim), lambda h, i: (h, 0, k_col)),
            pl.BlockSpec((1, length, head_dim), lambda h, i: (h, 0, v_col)),
            pl.BlockSpec((1, tile), lambda h, i: (0, i)),
            pl.BlockSpec((length, 1), lambda h, i: (0, 0)),
        ],
        out_specs=[block, block, row, row],
        out_shape=[
            jax.ShapeDtypeStruct((heads, queries, head_dim), BF16),
            jax.ShapeDtypeStruct((heads, queries, head_dim), F32),
            jax.ShapeDtypeStruct((heads, 1, queries), F32),
            jax.ShapeDtypeStruct((heads, 1, queries), F32),
        ],
        scratch_shapes=[pltpu.VMEM((head_dim, length), BF16)],
        compiler_params=pltpu.CompilerParams(vmem_limit_bytes=VMEM_LIMIT),
        cost_estimate=pl.CostEstimate(
            flops=4 * heads * queries * length * head_dim,
            bytes_accessed=heads * (queries + length) * head_dim * 8,
            transcendentals=heads * queries * length,
        ),
        name="attend",
    )(q_src, kv_src, kv_src, seg_q.reshape(1, -1), seg_k.reshape(-1, 1))


def attention_backward(q_src, kv_src, cols, grad, out_f32, lse, seg_q, seg_k, head_dim):
    heads, queries = q_src.shape[:2]
    length = kv_src.shape[1]
    tile = attention_tile(queries, length)
    q_col, k_col, v_col = cols
    scale = head_dim**-0.5
    row = pl.BlockSpec((1, 1, tile), lambda h, i: (h, 0, i))
    block = pl.BlockSpec((1, tile, head_dim), lambda h, i: (h, i, 0))
    whole = pl.BlockSpec((1, length, head_dim), lambda h, i: (h, 0, 0))
    return pl.pallas_call(
        functools.partial(attn_bwd_kernel, scale * LOG2E, scale),
        grid=(heads, queries // tile),
        in_specs=[
            pl.BlockSpec((1, tile, head_dim), lambda h, i: (h, i, q_col)),
            pl.BlockSpec((1, length, head_dim), lambda h, i: (h, 0, k_col)),
            pl.BlockSpec((1, length, head_dim), lambda h, i: (h, 0, v_col)),
            block,
            block,
            row,
            pl.BlockSpec((1, tile), lambda h, i: (0, i)),
            pl.BlockSpec((length, 1), lambda h, i: (0, 0)),
        ],
        out_specs=[block, whole, whole],
        out_shape=[
            jax.ShapeDtypeStruct((heads, queries, head_dim), BF16),
            jax.ShapeDtypeStruct((heads, length, head_dim), BF16),
            jax.ShapeDtypeStruct((heads, length, head_dim), BF16),
        ],
        scratch_shapes=[
            pltpu.VMEM((head_dim, length), BF16),
            pltpu.VMEM((length, head_dim), F32),
            pltpu.VMEM((length, head_dim), F32),
        ],
        compiler_params=pltpu.CompilerParams(vmem_limit_bytes=VMEM_LIMIT),
        cost_estimate=pl.CostEstimate(
            flops=10 * heads * queries * length * head_dim,
            bytes_accessed=heads * (queries + length) * head_dim * 12,
            transcendentals=heads * queries * length,
        ),
        name="attend_back",
    )(q_src, kv_src, kv_src, grad, out_f32, lse, seg_q.reshape(1, -1), seg_k.reshape(-1, 1))


def expert_step(expert, h_ref, ht_ref, dy_ref, dyt_ref, gate_ref, wg_ref, wu_ref, wd_ref, dg_ref, out_acc, dx_acc):
    width = h_ref.shape[1]
    cols = wg_ref.shape[3]
    w_gate = wg_ref[...].reshape(width, cols)
    w_up = wu_ref[...].reshape(width, cols)
    w_down = wd_ref[...].reshape(width, cols)
    gates = gate_ref[...]
    mine = lax.broadcasted_iota(jnp.int32, gates.shape, 1) == expert
    gate = jnp.sum(jnp.where(mine, gates, 0.0), axis=1, keepdims=True)
    a_gate = dot_nn(h_ref[...], w_gate)
    a_up = dot_nn(h_ref[...], w_up)
    raw = dot_nn(dy_ref[...], w_down)
    sigma = 1.0 / (1.0 + jnp.exp2(a_gate * -LOG2E))
    swish = a_gate * sigma
    act = swish * a_up
    dg_ref[0] += jnp.sum(raw * act, axis=1, keepdims=True)
    gated = (gate * act).astype(BF16)
    d_act = gate * raw
    d_gate = (d_act * a_up * (sigma + swish * (1.0 - sigma))).astype(BF16)
    d_up = (d_act * swish).astype(BF16)
    out_acc[...] += dot_nt(gated, w_down)
    dx_acc[...] += dot_nt(d_gate, w_gate) + dot_nt(d_up, w_up)
    for part, (left, right) in enumerate([(ht_ref, d_gate), (ht_ref, d_up), (dyt_ref, gated)]):
        yield part, dot_nn(left[...], right).astype(BF16)


def expert_kernel(more, counts, *refs):
    h_ref, ht_ref, dy_ref, dyt_ref, gate_ref = refs[:5]
    sources = [refs[5 + 3 * i : 8 + 3 * i] for i in range(len(counts))]
    out_ref, dx_ref, dg_ref, gr_ref, out_acc, dx_acc = refs[-6:]
    step, last = pl.program_id(0), pl.num_programs(0) - 1
    parts, _, part_rows, cols = sources[0][0].shape
    chunks = (last + 1) // sum(counts)

    @pl.when(step == 0)
    def _():
        if more:
            out0_ref, dx0_ref = refs[-8:-6]
            out_acc[...] = out0_ref[...].astype(F32)
            dx_acc[...] = dx0_ref[...].astype(F32)
        else:
            out_acc[...] = jnp.zeros_like(out_acc)
            dx_acc[...] = jnp.zeros_like(dx_acc)

    @pl.when(step % chunks == 0)
    def _():
        dg_ref[...] = jnp.zeros_like(dg_ref)

    begin = 0
    for source, count in zip(sources, counts):
        end = begin + count * chunks

        @pl.when((step >= begin) & (step < end))
        def _(source=source):
            for part, made in expert_step(
                step // chunks, h_ref, ht_ref, dy_ref, dyt_ref, gate_ref, *source, dg_ref, out_acc, dx_acc
            ):
                gr_ref[:, part, 0] = made.reshape(parts, part_rows, cols)

        begin = end

    @pl.when(step == last)
    def _():
        out_ref[...] = out_acc[...].astype(BF16)
        dx_ref[...] = dx_acc[...].astype(BF16)


def experts(hidden, hidden_t, grad, grad_t, gates, sources, before=()):
    tokens, width = hidden.shape
    parts, _, part_rows, units = sources[0][0].shape
    units = units // 3
    counts = [count for _, _, count in sources]
    total = sum(counts)
    cols = min(256, units)
    chunks = units // cols
    once = pl.Buffered(1)
    whole = pl.BlockSpec((tokens, width), lambda s: (0, 0), pipeline_mode=once)
    whole_t = pl.BlockSpec((width, tokens), lambda s: (0, 0), pipeline_mode=once)
    result = pl.BlockSpec((tokens, width), lambda s: (0, 0))

    def weight(source, kind):
        _, first, count = sources[source]
        begin = sum(counts[:source]) * chunks

        def index(step):
            at = jnp.clip(step - begin, 0, count * chunks - 1)
            return (0, first + at // chunks, 0, kind * chunks + at % chunks)

        return pl.BlockSpec((parts, 1, part_rows, cols), index)

    return pl.pallas_call(
        functools.partial(expert_kernel, bool(before), counts),
        grid=(total * chunks,),
        in_specs=[
            whole,
            whole_t,
            whole,
            whole_t,
            pl.BlockSpec(gates.shape, lambda s: (0, 0), pipeline_mode=once),
            *[weight(source, kind) for source in range(len(sources)) for kind in range(3)],
            *[whole for _ in before],
        ],
        out_specs=[
            result,
            result,
            pl.BlockSpec((1, tokens, 1), lambda s: (s // chunks, 0, 0)),
            pl.BlockSpec((parts, 3, 1, part_rows, cols), lambda s: (0, 0, s // chunks, 0, s % chunks)),
        ],
        out_shape=[
            jax.ShapeDtypeStruct((tokens, width), BF16),
            jax.ShapeDtypeStruct((tokens, width), BF16),
            jax.ShapeDtypeStruct((total, tokens, 1), F32),
            jax.ShapeDtypeStruct((parts, 3, total, part_rows, units), BF16),
        ],
        scratch_shapes=[
            pltpu.VMEM((tokens, width), F32),
            pltpu.VMEM((tokens, width), F32),
        ],
        compiler_params=pltpu.CompilerParams(vmem_limit_bytes=VMEM_LIMIT),
        cost_estimate=pl.CostEstimate(
            flops=18 * total * tokens * width * units,
            bytes_accessed=12 * total * width * units,
            transcendentals=total * tokens * units,
        ),
        name="experts",
    )(hidden, hidden_t, grad, grad_t, gates, *[array for array, _, _ in sources for _ in range(3)], *before)


def finish_experts_kernel(sums_ref, *refs):
    gate_up_ref, down_ref = refs[-2:]
    units = down_ref.shape[2]
    gate_up_ref[0, :, :units] = sums_ref[0, 0].astype(F32)
    gate_up_ref[0, :, units:] = sums_ref[1, 0].astype(F32)
    down_ref[0] = sums_ref[2, 0].astype(F32)


def finish_experts(sums, at, total, before=()):
    _, count, rows, units = sums.shape
    tile = min(128, rows)
    return pl.pallas_call(
        finish_experts_kernel,
        grid=(count, rows // tile),
        in_specs=[
            pl.BlockSpec((3, 1, tile, units), lambda e, r: (0, e, r, 0)),
            *[pl.BlockSpec(memory_space=pl.ANY) for _ in before],
        ],
        out_specs=[
            pl.BlockSpec((1, tile, 2 * units), lambda e, r: (at + e, r, 0)),
            pl.BlockSpec((1, tile, units), lambda e, r: (at + e, r, 0)),
        ],
        out_shape=[
            jax.ShapeDtypeStruct((total, rows, 2 * units), F32),
            jax.ShapeDtypeStruct((total, rows, units), F32),
        ],
        input_output_aliases={1 + i: i for i in range(len(before))},
        compiler_params=pltpu.CompilerParams(vmem_limit_bytes=VMEM_LIMIT),
        name="finish_experts",
    )(sums, *before)


def turn(values, cos, sin):
    return values * cos + pltpu.roll(values, values.shape[1] // 2, 1) * sin


def project_kernel(
    tok_ref, gain_ref, w_ref, cos_ref, sin_ref, gains_ref, hidden_ref, qkv_ref, raw_ref
):
    head_dim = cos_ref.shape[1]
    values = tok_ref[...].astype(F32)
    hidden = (values * rms_scale(values) * gain_ref[...]).astype(BF16)
    hidden_ref[...] = hidden
    projected = dot_nn(hidden, w_ref[...])
    raw_ref[...] = projected[:, : 2 * head_dim]
    for part in range(2):
        at = slice(part * head_dim, (part + 1) * head_dim)
        raw = projected[:, at]
        normed = raw * rms_scale(raw) * gains_ref[part : part + 1, :]
        qkv_ref[:, at] = turn(normed, cos_ref[...], sin_ref[...]).astype(BF16)
    qkv_ref[:, 2 * head_dim :] = projected[:, 2 * head_dim :].astype(BF16)


def project(toks, gain, weights, cos, sin, gains):
    length, width = toks.shape
    head_dim = cos.shape[1]
    tile = min(256, length)

    def rows(columns):
        return pl.BlockSpec((tile, columns), lambda i: (i, 0))

    def fixed(shape):
        return pl.BlockSpec(shape, lambda i: (0, 0))

    return pl.pallas_call(
        project_kernel,
        grid=(length // tile,),
        in_specs=[
            rows(width),
            fixed((1, width)),
            fixed(weights.shape),
            rows(head_dim),
            rows(head_dim),
            fixed(gains.shape),
        ],
        out_specs=[rows(width), rows(3 * head_dim), rows(2 * head_dim)],
        out_shape=[
            jax.ShapeDtypeStruct((length, width), BF16),
            jax.ShapeDtypeStruct((length, 3 * head_dim), BF16),
            jax.ShapeDtypeStruct((length, 2 * head_dim), F32),
        ],
        compiler_params=pltpu.CompilerParams(vmem_limit_bytes=VMEM_LIMIT),
        name="project",
    )(toks, gain, weights, cos, sin, gains)


def project_back_kernel(
    factor, scale, q_ref, k_ref, v_ref, do_ref, of_ref, lse_ref, sq_ref, sk_ref,
    raw_q_ref, raw_k_ref, cos_q_ref, sin_q_ref, cos_ref, sin_ref, gains_ref,
    dp_ref, dgain_ref, kt_ref, dk_acc, dv_acc,
):
    length, head_dim = k_ref.shape
    size, count = key_chunks(length)
    tile = q_ref.shape[0]
    step_at = pl.program_id(0)

    @pl.when(step_at == 0)
    def _():
        kt_ref[...] = k_ref[...].astype(F32).T.astype(BF16)
        dk_acc[...] = jnp.zeros_like(dk_acc)
        dv_acc[...] = jnp.zeros_like(dv_acc)
        dgain_ref[...] = jnp.zeros_like(dgain_ref)

    def to_raw(part, grad, raw, cos, sin):
        grad = turn(grad.astype(BF16).astype(F32), cos, -sin)
        raw_scale = rms_scale(raw)
        dgain_ref[part : part + 1, :] += jnp.sum(grad * (raw * raw_scale), axis=0, keepdims=True)
        return norm_back(grad * gains_ref[part : part + 1, :], raw, raw_scale).astype(BF16)

    q = q_ref[...]
    grad = do_ref[...]
    seg_q = sq_ref[...]
    lse = lse_ref[0]
    row_dot = jnp.sum((grad.astype(F32) * of_ref[0]).T, axis=0, keepdims=True)
    dq_t = jnp.zeros((head_dim, tile), F32)
    for j in range(count):
        rows = slice(j * size, (j + 1) * size)
        scores = dot_nt(k_ref[rows, :], q)
        scores = jnp.where(sk_ref[rows, :] == seg_q, scores, NEG)
        weights = jnp.exp2(scores * factor - lse)
        grad_weights = dot_nt(v_ref[rows, :], grad)
        grad_scores = (weights * (grad_weights - row_dot)).astype(BF16)
        dk_acc[rows, :] += dot_nn(grad_scores, q)
        dv_acc[rows, :] += dot_nn(weights.astype(BF16), grad)
        dq_t = dq_t + dot_nn(kt_ref[:, rows], grad_scores)
    own = pl.ds(pl.multiple_of(step_at * tile, tile), tile)
    dp_ref[own, :head_dim] = to_raw(
        0, (dq_t * scale).T, raw_q_ref[...], cos_q_ref[...], sin_q_ref[...]
    )

    @pl.when(step_at == pl.num_programs(0) - 1)
    def _():
        dp_ref[:, head_dim : 2 * head_dim] = to_raw(
            1, dk_acc[...] * scale, raw_k_ref[...], cos_ref[...], sin_ref[...]
        )
        dp_ref[:, 2 * head_dim :] = dv_acc[...].astype(BF16)


def project_back(qkv, grad, out_f32, lse, segments, raw, cos, sin, gains):
    length, head_dim = grad.shape
    tile = min(256, length)

    def rows(column):
        return pl.BlockSpec((tile, head_dim), lambda i: (i, column))

    def whole(column):
        return pl.BlockSpec((length, head_dim), lambda i: (0, column))

    return pl.pallas_call(
        functools.partial(project_back_kernel, head_dim**-0.5 * LOG2E, head_dim**-0.5),
        grid=(length // tile,),
        in_specs=[
            rows(0),
            whole(1),
            whole(2),
            rows(0),
            pl.BlockSpec((1, tile, head_dim), lambda i: (0, i, 0)),
            pl.BlockSpec((1, 1, tile), lambda i: (0, 0, i)),
            pl.BlockSpec((1, tile), lambda i: (0, i)),
            pl.BlockSpec((length, 1), lambda i: (0, 0)),
            rows(0),
            whole(1),
            rows(0),
            rows(0),
            whole(0),
            whole(0),
            pl.BlockSpec(gains.shape, lambda i: (0, 0)),
        ],
        out_specs=[
            pl.BlockSpec((length, 3 * head_dim), lambda i: (0, 0)),
            pl.BlockSpec((2, head_dim), lambda i: (0, 0)),
        ],
        out_shape=[
            jax.ShapeDtypeStruct((length, 3 * head_dim), BF16),
            jax.ShapeDtypeStruct((2, head_dim), F32),
        ],
        scratch_shapes=[
            pltpu.VMEM((head_dim, length), BF16),
            pltpu.VMEM((length, head_dim), F32),
            pltpu.VMEM((length, head_dim), F32),
        ],
        compiler_params=pltpu.CompilerParams(vmem_limit_bytes=VMEM_LIMIT),
        cost_estimate=pl.CostEstimate(
            flops=10 * length * length * head_dim,
            bytes_accessed=length * head_dim * 40,
            transcendentals=length * length,
        ),
        name="project_back",
    )(
        qkv, qkv, qkv, grad, out_f32, lse, segments.reshape(1, -1), segments.reshape(-1, 1),
        raw, raw, cos, sin, cos, sin, gains,
    )


def hidden_back_kernel(grads_ref, own_ref, near_ref, far_ref, cross_ref, hidden_ref, out_ref, gain_ref):
    uly = grads_ref.shape[0]
    u = lax.axis_index(ULY)
    near = u + 1 - 2 * lax.rem(u, 2)
    total = dot_nt(grads_ref[u], own_ref[...])
    total = total + dot_nt(grads_ref[near], near_ref[...])
    total = total + dot_nt(grads_ref[lax.rem(u + 2, uly)], far_ref[...])
    total = total + dot_nt(grads_ref[lax.rem(near + 2, uly)], cross_ref[...])
    out_ref[...] = total.astype(BF16).reshape(out_ref.shape)
    hidden = hidden_ref[...].reshape(total.shape).astype(F32)
    gain_ref[...] = jnp.sum(total * hidden, axis=0, keepdims=True)


def hidden_back(grads, own, near, far, cross, hidden):
    uly, tokens, columns = grads.shape
    blk, _, rows, width = hidden.shape
    tile = min(512, width)
    weights = pl.BlockSpec((tile, columns), lambda n: (n, 0))
    return pl.pallas_call(
        hidden_back_kernel,
        grid=(width // tile,),
        in_specs=[
            pl.BlockSpec(grads.shape, lambda n: (0, 0, 0)),
            *[weights] * 4,
            pl.BlockSpec((blk, 1, rows, tile), lambda n: (0, lax.axis_index(ULY), 0, n)),
        ],
        out_specs=[
            pl.BlockSpec((blk, rows, tile), lambda n: (0, 0, n)),
            pl.BlockSpec((1, tile), lambda n: (0, n)),
        ],
        out_shape=[
            jax.ShapeDtypeStruct((blk, rows, width), BF16),
            jax.ShapeDtypeStruct((1, width), F32),
        ],
        compiler_params=pltpu.CompilerParams(vmem_limit_bytes=VMEM_LIMIT),
        name="hidden_back",
    )(grads, own, near, far, cross, hidden)


def merge_heads_kernel(parts_ref, out_ref):
    blk, uly, _, columns = parts_ref.shape
    head_dim = columns // 3
    heads = blk * uly
    for z in range(blk):
        for u in range(uly):
            head = parts_ref[z, u].astype(F32)
            for part in range(3):
                at = (part * heads + u * blk + z) * head_dim
                out_ref[:, at : at + head_dim] = head[:, part * head_dim : (part + 1) * head_dim]


def merge_heads(parts):
    blk, uly, rows, columns = parts.shape
    return pl.pallas_call(
        merge_heads_kernel,
        out_shape=jax.ShapeDtypeStruct((rows, blk * uly * columns), F32),
        compiler_params=pltpu.CompilerParams(vmem_limit_bytes=VMEM_LIMIT),
        name="merge_heads",
    )(parts)


def swap(values, axis):
    return lax.all_to_all(values, axis, split_axis=0, concat_axis=0, tiled=True)


def sum_scatter(values, axis):
    count = spread(axis) if isinstance(axis, tuple) else lax.axis_size(axis)
    rows, width = values.shape
    parts = swap(values.astype(BF16).reshape(count, rows // count, width), axis)
    return jnp.sum(parts.astype(F32), axis=0)


def place(axes, index):
    found = {}
    for axis in reversed(axes):
        size = lax.axis_size(axis)
        found[axis] = lax.rem(index, size)
        index = index // size
    return found


def spread(axes):
    return math.prod(lax.axis_size(axis) for axis in axes)


def each(count, body):
    if count <= 4:
        for step in range(1, count):
            body(step)
    else:

        def looped(step, carried):
            body(step)
            return carried

        lax.fori_loop(1, count, looped, 0)


def ahead(index, step, size):
    return lax.rem(index + step, size)


def exchange(items, collective_id, after=()):
    count = len(items)
    sizes = [spread(axes) for _, axes, _ in items]
    groups = list(dict.fromkeys(axes for _, axes, _ in items))
    bases = [sum(2 * size for size in sizes[:i]) for i in range(count)]

    def kernel(*refs):
        ins = refs[:count]
        outs = refs[count + len(after) : 2 * count + len(after)]
        send, recv, local = refs[2 * count + len(after) :][:3]
        barrier = pltpu.get_barrier_semaphore()
        for axes in groups:
            size, me = spread(axes), lax.axis_index(axes)

            def greet(step, axes=axes, size=size, me=me):
                pl.semaphore_signal(
                    barrier, inc=1, device_id=place(axes, ahead(me, step, size)), device_id_type=MESH
                )

            each(size, greet)
        pl.semaphore_wait(barrier, sum(spread(axes) - 1 for axes in groups))

        def block(i, peer):
            if items[i][2] == "swap":
                return ins[i].at[peer]
            return ins[i].at[:, peer] if items[i][2] == "swap1" else ins[i]

        def remote(i, step):
            _, axes, kind = items[i]
            me = lax.axis_index(axes)
            if kind == "trade":
                return pltpu.make_async_remote_copy(
                    src_ref=ins[i],
                    dst_ref=outs[i],
                    send_sem=send.at[bases[i] + 1],
                    recv_sem=recv.at[bases[i] + 1],
                    device_id=place(axes, 1 - me),
                    device_id_type=MESH,
                )
            if kind == "relay":
                far, near = lax.rem(me + 2, 4), me + 1 - 2 * lax.rem(me, 2)
                held = far if step == 3 else me
                return pltpu.make_async_remote_copy(
                    src_ref=outs[i].at[far] if step == 3 else ins[i],
                    dst_ref=outs[i].at[held],
                    send_sem=send.at[bases[i] + step],
                    recv_sem=recv.at[bases[i] + step],
                    device_id=place(axes, far if step == 1 else near),
                    device_id_type=MESH,
                )
            peer = ahead(me, step, sizes[i])
            return pltpu.make_async_remote_copy(
                src_ref=block(i, peer),
                dst_ref=outs[i].at[me],
                send_sem=send.at[bases[i] + step],
                recv_sem=recv.at[bases[i] + step],
                device_id=place(axes, peer),
                device_id_type=MESH,
            )

        def own(i):
            _, axes, kind = items[i]
            me = lax.axis_index(axes)
            return pltpu.make_async_copy(
                block(i, me), outs[i].at[me], local.at[i]
            )

        def hop(i, up, hops):
            (axis,) = items[i][1]
            me, size = lax.axis_index(axis), sizes[i]
            way = 1 if up else -1
            held, to = me - way * hops, me + way
            exists = (held >= 0) & (held < size) & (to >= 0) & (to < size)
            held, to = jnp.clip(held, 0, size - 1), jnp.clip(to, 0, size - 1)
            sem = bases[i] + (size if up else 0) + hops
            copy = pltpu.make_async_remote_copy(
                src_ref=outs[i].at[held] if hops else ins[i],
                dst_ref=outs[i].at[held],
                send_sem=send.at[sem],
                recv_sem=recv.at[sem],
                device_id={axis: to},
                device_id_type=MESH,
            )
            return exists, copy

        def arrival(i, up, hops):
            (axis,) = items[i][1]
            me, size = lax.axis_index(axis), sizes[i]
            way = 1 if up else -1
            held, sender = me - way * (hops + 1), me - way
            exists = (held >= 0) & (held < size)
            held, sender = jnp.clip(held, 0, size - 1), jnp.clip(sender, 0, size - 1)
            sem = bases[i] + (size if up else 0) + hops
            copy = pltpu.make_async_remote_copy(
                src_ref=ins[i],
                dst_ref=outs[i].at[held],
                send_sem=send.at[sem],
                recv_sem=recv.at[sem],
                device_id={axis: sender},
                device_id_type=MESH,
            )
            return exists, copy

        def kinds(*names):
            return [i for i in range(count) if items[i][2] in names]

        def when(pair, act):
            exists, copy = pair
            pl.when(exists)(lambda: act(copy))

        def pairsum(i):
            me = lax.axis_index(ULY)
            far, near = lax.rem(me + 2, 4), me + 1 - 2 * lax.rem(me, 2)
            own, out = ins[i], outs[i]
            got_near, got_far, sent = refs[2 * count + len(after) + 3 :]

            def copy(at, src, dst, to):
                return pltpu.make_async_remote_copy(
                    src_ref=src,
                    dst_ref=dst,
                    send_sem=send.at[bases[i] + at],
                    recv_sem=recv.at[bases[i] + at],
                    device_id=place(ULY, to),
                    device_id_type=MESH,
                )

            to_near = [
                copy(0, own.at[near], got_near.at[0], near),
                copy(1, own.at[lax.rem(near + 2, 4)], got_near.at[1], near),
            ]
            to_far = copy(2, sent, got_far, far)

            def first():
                for sending in to_near:
                    sending.start()

            def second():
                for sending in to_near:
                    sending.wait()
                sent[...] = (own[far].astype(F32) + got_near[1].astype(F32)).astype(BF16)
                to_far.start()
                out[...] = own[me].astype(F32) + got_near[0].astype(F32)

            def third():
                to_far.wait()
                out[...] += got_far[...].astype(F32)

            return first, second, third

        ways = (True, False)
        sums = [pairsum(i) for i in kinds("pairsum")]
        for first, _, _ in sums:
            first()
        for i in kinds("line"):
            for up in ways:
                when(hop(i, up, 0), lambda copy: copy.start())
        for i in kinds("gather", "swap", "swap1", "relay", "trade"):
            each(3 if items[i][2] == "relay" else sizes[i], lambda step, i=i: remote(i, step).start())
        for i in kinds("gather", "swap", "swap1", "relay", "line"):
            own(i).start()
        for _, second, _ in sums:
            second()
        for i in kinds("line"):
            for hops in range(1, sizes[i]):
                for up in ways:
                    when(arrival(i, up, hops - 1), lambda copy: copy.wait_recv())
                    if hops < sizes[i] - 1:
                        when(hop(i, up, hops), lambda copy: copy.start())
        for i in kinds("relay"):
            remote(i, 1).wait_recv()
            remote(i, 3).start()
            remote(i, 1).wait_send()
            for step in (2, 3):
                remote(i, step).wait()
        for i in kinds("gather", "swap", "swap1", "trade"):
            each(sizes[i], lambda step, i=i: remote(i, step).wait())
        for i in kinds("line"):
            for hops in range(sizes[i] - 1):
                for up in ways:
                    when(hop(i, up, hops), lambda copy: copy.wait_send())
        for i in kinds("gather", "swap", "swap1", "relay", "line"):
            own(i).wait()
        for _, _, third in sums:
            third()


    def shape_of(size, array, kind):
        if kind in ("trade", "pairsum"):
            return array.shape[kind == "pairsum" :]
        dropped = {"swap": 0, "swap1": 1}.get(kind)
        return (size, *(extent for at, extent in enumerate(array.shape) if at != dropped))

    anywhere, close = pl.BlockSpec(memory_space=pl.ANY), pl.BlockSpec(memory_space=pltpu.VMEM)
    specs = [close if kind == "pairsum" else anywhere for _, _, kind in items]
    held = []
    for array, _, kind in items:
        if kind == "pairsum":
            held = [pltpu.VMEM((*more, *array.shape[1:]), BF16) for more in ((2,), (), ())]
    return pl.pallas_call(
        kernel,
        in_specs=specs + [anywhere] * len(after),
        out_specs=specs,
        out_shape=[
            jax.ShapeDtypeStruct(shape_of(size, array, kind), F32 if kind == "pairsum" else array.dtype)
            for size, (array, _, kind) in zip(sizes, items)
        ],
        scratch_shapes=[
            pltpu.SemaphoreType.DMA((2 * sum(sizes),)),
            pltpu.SemaphoreType.DMA((2 * sum(sizes),)),
            pltpu.SemaphoreType.DMA((count,)),
            *held,
        ],
        compiler_params=pltpu.CompilerParams(
            collective_id=collective_id, has_side_effects=True, vmem_limit_bytes=VMEM_LIMIT if held else None
        ),
        name="exchange",
    )(*[item[0] for item in items], *after)


def turn_gather_kernel(
    own_ref, other_ref, all_ref, all_t_ref, other_t_ref, block, turned, send, recv, local
):
    size, me = lax.axis_size("blk"), lax.axis_index("blk")
    rows = own_ref.shape[0]
    barrier = pltpu.get_barrier_semaphore()
    ways = (1, 0)

    def neighbour(up):
        to = me + (1 if up else -1)
        return (to >= 0) & (to < size), jnp.clip(to, 0, size - 1)

    def greet(step):
        pl.semaphore_signal(
            barrier, inc=1, device_id={"blk": ahead(me, step, size)}, device_id_type=MESH
        )

    each(size, greet)
    pl.semaphore_wait(barrier, size - 1)

    def hop(up, hops):
        held = me - (1 if up else -1) * hops
        exists, to = neighbour(up)
        exists = exists & (held >= 0) & (held < size)
        held = jnp.clip(held, 0, size - 1)
        return exists, pltpu.make_async_remote_copy(
            src_ref=all_ref.at[held] if hops else own_ref,
            dst_ref=all_ref.at[held],
            send_sem=send.at[up * size + hops],
            recv_sem=recv.at[up * size + hops],
            device_id={"blk": to},
            device_id_type=MESH,
        )

    def arrival(up, hops):
        held = me - (1 if up else -1) * (hops + 1)
        exists = (held >= 0) & (held < size)
        held = jnp.clip(held, 0, size - 1)
        return exists, held, pltpu.make_async_remote_copy(
            src_ref=own_ref,
            dst_ref=all_ref.at[held],
            send_sem=send.at[up * size + hops],
            recv_sem=recv.at[up * size + hops],
            device_id={"blk": neighbour(1 - up)[1]},
            device_id_type=MESH,
        )

    def when(pair, act):
        exists, copy = pair
        pl.when(exists)(lambda: act(copy))

    def turn(src, dst, at):
        take = pltpu.make_async_copy(src, block, local.at[0])
        take.start()
        take.wait()
        turned[...] = block[...].T
        columns = pl.ds(pl.multiple_of(at * rows, rows), rows)
        give = pltpu.make_async_copy(turned, dst.at[:, columns], local.at[1])
        give.start()
        give.wait()

    for up in ways:
        when(hop(up, 0), lambda copy: copy.start())
    keep = pltpu.make_async_copy(own_ref, all_ref.at[me], local.at[2])
    keep.start()
    turn(own_ref, all_t_ref, me)
    for at in range(size):
        turn(other_ref.at[at], other_t_ref, at)
    for hops in range(1, size):
        for up in ways:
            exists, held, copy = arrival(up, hops - 1)

            @pl.when(exists)
            def _(copy=copy, up=up, hops=hops):
                copy.wait_recv()
                if hops < size - 1:
                    when(hop(up, hops), lambda copy: copy.start())

        for up in ways:
            exists, held, copy = arrival(up, hops - 1)
            pl.when(exists)(lambda held=held: turn(all_ref.at[held], all_t_ref, held))
    for hops in range(size - 1):
        for up in ways:
            when(hop(up, hops), lambda copy: copy.wait_send())
    keep.wait()


def turn_gather(own, other, collective_id, after=()):
    size = lax.axis_size("blk")
    rows, width = own.shape
    anywhere = pl.BlockSpec(memory_space=pl.ANY)

    def kernel(*refs):
        turn_gather_kernel(*refs[:2], *refs[2 + len(after) :])

    return pl.pallas_call(
        kernel,
        in_specs=[anywhere] * (2 + len(after)),
        out_specs=[anywhere] * 3,
        out_shape=[
            jax.ShapeDtypeStruct((size, rows, width), BF16),
            jax.ShapeDtypeStruct((width, size * rows), BF16),
            jax.ShapeDtypeStruct((width, size * rows), BF16),
        ],
        scratch_shapes=[
            pltpu.VMEM((rows, width), BF16),
            pltpu.VMEM((width, rows), BF16),
            pltpu.SemaphoreType.DMA((2 * size,)),
            pltpu.SemaphoreType.DMA((2 * size,)),
            pltpu.SemaphoreType.DMA((3,)),
        ],
        compiler_params=pltpu.CompilerParams(
            collective_id=collective_id, has_side_effects=True, vmem_limit_bytes=VMEM_LIMIT
        ),
        name="turn_gather",
    )(own, other, *after)


def startup_kernel(
    head_ref, extra_ref, tok_ref, heads_ref, extras_ref, toks_ref,
    head_send, head_recv, extra_send, extra_recv, trade_send, trade_recv,
    z_send, z_recv, ay_send, ay_recv, by_send, by_recv, c_send, c_recv, local,
):
    blk, uly = lax.axis_size("blk"), spread(ULY)
    total = spread(ALL)
    z, u, me = lax.axis_index("blk"), lax.axis_index(ULY), lax.axis_index(ALL)
    far = lax.rem(u + 2, uly)
    near = u + 1 - 2 * lax.rem(u, 2)
    half = tok_ref.shape[0] // 2
    parts = (pl.ds(0, half), pl.ds(half, half))

    barrier = pltpu.get_barrier_semaphore()

    def greet(step):
        pl.semaphore_signal(
            barrier, inc=1, device_id=place(ALL, ahead(me, step, total)), device_id_type=MESH
        )

    each(total, greet)
    pl.semaphore_wait(barrier, total - 1)

    def send(src, dst, sent, got, to):
        return pltpu.make_async_remote_copy(
            src_ref=src, dst_ref=dst, send_sem=sent, recv_sem=got, device_id=to, device_id_type=MESH
        )

    def block(step, other, part):
        at = toks_ref.at[ahead(z, step, blk), far if other else u, parts[part]]
        return (tok_ref.at[parts[part]] if step == 0 and not other else at), at

    streams = ((0, 0), (0, 1), (1, 1))

    def hop(stream, up, hops):
        other, part = streams[stream]
        way = 1 if up else -1
        held, to = z - way * hops, z + way
        exists = (held >= 0) & (held < blk) & (to >= 0) & (to < blk)
        held, to = jnp.clip(held, 0, blk - 1), jnp.clip(to, 0, blk - 1)
        at = toks_ref.at[held, far if other else u, parts[part]]
        src = tok_ref.at[parts[part]] if hops == 0 and not other else at
        sem = (2 * stream + up) * blk + hops
        return exists, send(src, at, z_send.at[sem], z_recv.at[sem], {"blk": to})

    def arrival(stream, up, hops):
        other, part = streams[stream]
        way = 1 if up else -1
        held, sender = z - way * (hops + 1), z - way
        exists = (held >= 0) & (held < blk)
        held, sender = jnp.clip(held, 0, blk - 1), jnp.clip(sender, 0, blk - 1)
        at = toks_ref.at[held, far if other else u, parts[part]]
        sem = (2 * stream + up) * blk + hops
        return exists, send(tok_ref.at[parts[part]], at, z_send.at[sem], z_recv.at[sem], {"blk": sender})

    def when(pair, act):
        exists, copy = pair
        pl.when(exists)(lambda: act(copy))

    def a_y(step):
        return send(*block(step, 0, 0), ay_send.at[step], ay_recv.at[step], place(ULY, far))

    def b_y():
        return send(*block(0, 0, 1), by_send.at[0], by_recv.at[0], place(ULY, far))

    def to_near(step, other, part):
        sem = 4 * step + 2 * other + part
        return send(*block(step, other, part), c_send.at[sem], c_recv.at[sem], place(ULY, near))

    group = ("blk", *ULY)
    mine, here, b = lax.axis_index(group), spread(group), lax.axis_index("batch")

    def head(step):
        to = place(group, ahead(mine, step, here))
        src = head_ref.at[(to["y"] * lax.axis_size("core") + to["core"]) * blk + to["blk"]]
        return send(src, heads_ref.at[b, mine], head_send.at[step], head_recv.at[step], to)

    def extra(step):
        to = place(group, ahead(mine, step, here))
        return send(extra_ref, extras_ref.at[b, mine], extra_send.at[step], extra_recv.at[step], to)

    def trade(which):
        ref = (heads_ref, extras_ref)[which].at[b]
        return send(ref, ref, trade_send.at[which], trade_recv.at[which], {"batch": 1 - b})

    own = [
        pltpu.make_async_copy(tok_ref, toks_ref.at[z, u], local.at[0]),
        pltpu.make_async_copy(head_ref.at[u * blk + z], heads_ref.at[b, mine], local.at[1]),
        pltpu.make_async_copy(extra_ref, extras_ref.at[b, mine], local.at[2]),
    ]

    def start_head(step):
        extra(step).start()
        head(step).start()

    each(here, start_head)
    ways = (1, 0)
    b_y().start()
    for stream in range(2):
        for up in ways:
            when(hop(stream, up, 0), lambda copy: copy.start())
    a_y(0).start()
    to_near(0, 0, 0).start()
    to_near(0, 0, 1).start()

    for copy in own:
        copy.start()
    b_y().wait_recv()
    for up in ways:
        when(hop(2, up, 0), lambda copy: copy.start())
    to_near(0, 1, 1).start()
    def wait_head(step):
        extra(step).wait()
        head(step).wait()

    for hops in range(1, blk):
        if hops == min(2, blk - 1):
            each(here, wait_head)
            for copy in own[1:]:
                copy.wait()
            trade(0).start()
            trade(1).start()
        for stream, (other, part) in enumerate(streams):
            for up in ways:
                exists, copy = arrival(stream, up, hops - 1)
                step = blk - hops if up else hops

                @pl.when(exists)
                def _(copy=copy, stream=stream, other=other, part=part, up=up, step=step, hops=hops):
                    copy.wait_recv()
                    if hops < blk - 1:
                        when(hop(stream, up, hops), lambda copy: copy.start())
                    if stream == 0:
                        a_y(step).start()
                    to_near(step, other, part).start()

    for step in [0, *reversed(range(1, blk))]:
        a_y(step).wait_recv()
        to_near(step, 1, 0).start()
    for step in range(blk):
        for other in range(2):
            for part in range(2):
                to_near(step, other, part).wait_recv()

    trade(0).wait()
    trade(1).wait()
    own[0].wait()
    b_y().wait_send()
    for hops in range(blk - 1):
        for stream in range(3):
            for up in ways:
                when(hop(stream, up, hops), lambda copy: copy.wait_send())
    for step in range(blk):
        a_y(step).wait_send()
        for other in range(2):
            for part in range(2):
                to_near(step, other, part).wait_send()


def startup(heads, extra, tok, collective_id):
    batch, blk, uly = lax.axis_size("batch"), lax.axis_size("blk"), spread(ULY)
    anywhere = pl.BlockSpec(memory_space=pl.ANY)
    dma = pltpu.SemaphoreType.DMA
    return pl.pallas_call(
        startup_kernel,
        in_specs=[anywhere] * 3,
        out_specs=[anywhere] * 3,
        out_shape=[
            jax.ShapeDtypeStruct((batch, blk * uly, *heads.shape[1:]), BF16),
            jax.ShapeDtypeStruct((batch, blk * uly, *extra.shape), BF16),
            jax.ShapeDtypeStruct((blk, uly, *tok.shape), BF16),
        ],
        scratch_shapes=[
            *[dma((blk * uly,))] * 4,
            *[dma((2,))] * 2,
            *[dma((6 * blk,))] * 2,
            *[dma((blk,))] * 2,
            *[dma((1,))] * 2,
            *[dma((4 * blk,))] * 2,
            dma((3,)),
        ],
        compiler_params=pltpu.CompilerParams(collective_id=collective_id, has_side_effects=True),
        name="startup",
    )(heads, extra, tok)


def per_device_general(
    tokens, segments, routes, w_qkv, w_out, attn_gain, ffn_gain, qk_gain, router, w_gate_up, w_down, cotangent
):
    own_tokens = tokens[0]
    own_grad = cotangent[0]
    count_tok, width = own_tokens.shape
    head_dim = qk_gain.shape[1]
    heads = width // head_dim
    uly, blk, batch = spread(ULY), lax.axis_size("blk"), lax.axis_size("batch")
    blk_at, uly_at = lax.axis_index("blk"), lax.axis_index(ULY)
    group = batch * blk
    local_heads = heads // uly
    local_width = local_heads * head_dim
    rows = count_tok * uly
    seg_row = segments[0]
    length = seg_row.shape[0]
    number = router.shape[1]
    local_experts, _, units = w_down.shape
    shard_rows = w_qkv.shape[0]

    extra = jnp.concatenate([attn_gain[:, None], ffn_gain[:, None], router], axis=1)
    extra = jnp.pad(extra, ((0, 0), (0, LANES - extra.shape[1])))
    columns = w_qkv.reshape(shard_rows, 3, uly, local_width).transpose(2, 0, 1, 3)
    packed = jnp.concatenate(
        [
            columns.reshape(uly, shard_rows, 3 * local_width),
            jnp.broadcast_to(extra[None], (uly, shard_rows, LANES)),
        ],
        axis=2,
    )
    packed = swap(packed, ULY).reshape(uly * shard_rows, 3 * local_width + LANES)
    packed = lax.all_gather(packed, ROWS, axis=0, tiled=True)
    own_qkv = packed[:, : 3 * local_width]
    gain_attn = packed[:, 3 * local_width].astype(F32)
    gain_ffn = packed[:, 3 * local_width + 1].astype(F32)
    whole_router = packed[:, 3 * local_width + 2 : 3 * local_width + 2 + number]
    tokens_all = lax.all_gather(own_tokens, ULY, axis=0, tiled=True)
    to_rows = [(u * group + g, g * uly + u) for g in range(group) for u in range(uly)]
    own_out = lax.all_gather(lax.ppermute(w_out, ALL, to_rows), ROWS, axis=0, tiled=True)
    whole_gate_up = lax.all_gather(w_gate_up, PLANE, axis=0, tiled=False)
    whole_down = lax.all_gather(w_down, PLANE, axis=0, tiled=False)
    grad_blk = lax.all_gather(own_grad, "blk", axis=0, tiled=True)
    routes_blk = lax.all_gather(routes[0], "blk", axis=0, tiled=True)

    gain_query = qk_gain[0].astype(F32)
    gain_key = qk_gain[1].astype(F32)
    inputs_all = tokens_all.astype(F32)
    normed_one = inputs_all * rms_scale(inputs_all)
    hidden_one = (normed_one * gain_attn).astype(BF16)
    projected = dot_nn(hidden_one, own_qkv)
    query_raw = projected[:, :local_width].reshape(rows, local_heads, head_dim)
    key_raw = projected[:, local_width : 2 * local_width].reshape(rows, local_heads, head_dim)
    value_raw = projected[:, 2 * local_width :].reshape(rows, local_heads, head_dim)
    cos_table, sin_table = rope_tables(blk_at * rows, rows, head_dim)
    query_scale = rms_scale(query_raw)
    key_scale = rms_scale(key_raw)
    qkv = jnp.concatenate(
        [
            rotate(query_raw * query_scale * gain_query, cos_table, sin_table),
            rotate(key_raw * key_scale * gain_key, cos_table, sin_table),
            value_raw,
        ],
        axis=2,
    ).astype(BF16)
    qkv = qkv.transpose(1, 0, 2)

    by_heads = local_heads % blk == 0
    if by_heads:
        per = local_heads // blk

        def to_heads(values):
            columns = values.shape[2]
            moved = swap(values.reshape(blk, per, rows, columns), "blk")
            return moved.transpose(1, 0, 2, 3).reshape(per, length, columns)

        def to_rows_back(values):
            columns = values.shape[2]
            parts = values.reshape(per, blk, rows, columns).transpose(1, 0, 2, 3)
            return swap(parts, "blk").reshape(local_heads, rows, columns)

        q_src = kv_src = to_heads(qkv)
        cols = (0, 1, 2)
        seg_q = seg_row
        first_head = uly_at * local_heads + blk_at * per
    else:

        def to_heads(values):
            return values

        def to_rows_back(values):
            return values

        q_src = qkv
        kv_src = lax.all_gather(qkv[:, :, head_dim:], "blk", axis=1, tiled=True)
        cols = (0, 0, 1)
        seg_q = lax.dynamic_slice_in_dim(seg_row, blk_at * rows, rows)
        first_head = uly_at * local_heads
    attn_low, attn_f32, lse, top = attention_forward(q_src, kv_src, cols, seg_q, seg_row, head_dim)
    head_vector = lax.dynamic_update_slice_in_dim(
        jnp.full((heads,), NEG, F32), jnp.max(top, axis=(1, 2)) * head_dim**-0.5, first_head, 0
    )
    head_max = lax.pmax(head_vector, ALL)
    attn_rows = to_rows_back(attn_low)
    out_heads = own_out.reshape(local_heads, head_dim, width)
    branch = jnp.einsum("htc,hcd->td", attn_rows, out_heads, preferred_element_type=F32)
    inputs = own_tokens.astype(F32)
    mid = inputs + sum_scatter(branch, ULY)

    scale_two = rms_scale(mid)
    normed_two = mid * scale_two
    hidden_two = (normed_two * gain_ffn).astype(BF16)
    hidden_blk = lax.all_gather(hidden_two, "blk", axis=0, tiled=True)
    probs_blk = jax.nn.softmax(dot_nn(hidden_blk, whole_router), axis=1)
    names = jnp.arange(number, dtype=jnp.int32)
    chosen_blk = jnp.any(routes_blk[:, :, None] == names, axis=1).astype(F32)
    own_names = blk_at * local_experts
    gates = lax.dynamic_slice_in_dim(probs_blk * chosen_blk, own_names, local_experts, axis=1)
    most = min(MOST_TOKENS, hidden_blk.shape[0])
    packed_weights = jnp.concatenate([whole_gate_up, whole_down], axis=3)
    made = []
    for at in range(0, hidden_blk.shape[0], most):
        hidden_part, grad_part = hidden_blk[at : at + most], grad_blk[at : at + most]
        made.append(
            experts(
                hidden_part,
                hidden_part.T,
                grad_part,
                grad_part.T,
                gates[at : at + most],
                [(packed_weights, 0, local_experts)],
            )
        )
    out_part = jnp.concatenate([m[0] for m in made], axis=0)
    dx_part = jnp.concatenate([m[1] for m in made], axis=0)
    dg_part = jnp.concatenate([m[2] for m in made], axis=1)
    expert_grads = sum(m[3].astype(F32) for m in made).astype(BF16)
    expert_sums = lax.psum_scatter(expert_grads, PLANE, scatter_dimension=0, tiled=False).astype(F32)
    grad_gate_up = jnp.concatenate([expert_sums[0], expert_sums[1]], axis=2)
    grad_down = expert_sums[2]
    dg_parts = swap(dg_part.reshape(local_experts, blk, count_tok).transpose(1, 2, 0), "blk")
    grad_gates = dg_parts.transpose(1, 0, 2).reshape(count_tok, number)
    dx_sum = sum_scatter(dx_part, "blk")
    output = (mid + sum_scatter(out_part, "blk")).astype(BF16)
    router_probs = lax.dynamic_slice_in_dim(probs_blk, blk_at * count_tok, count_tok)
    chosen = lax.dynamic_slice_in_dim(chosen_blk, blk_at * count_tok, count_tok)
    grad_probs = chosen * grad_gates
    grad_logits = (
        router_probs * (grad_probs - jnp.sum(router_probs * grad_probs, axis=1, keepdims=True))
    ).astype(BF16)
    grad_hidden_two = dx_sum + dot_nt(grad_logits, whole_router)
    grad_router_part = dot_tn(hidden_two, grad_logits)
    grad_gain_ffn = jnp.sum(grad_hidden_two * normed_two, axis=0)
    grad_mid = own_grad.astype(F32) + norm_back(grad_hidden_two * gain_ffn, mid, scale_two)

    branch_grad = lax.all_gather(grad_mid.astype(BF16), ULY, axis=0, tiled=True)
    grad_attn = dot_nt(branch_grad, own_out).astype(BF16)
    grad_attn = to_heads(grad_attn.reshape(rows, local_heads, head_dim).transpose(1, 0, 2))
    grad_out_part = jnp.einsum("htc,td->hcd", attn_rows, branch_grad, preferred_element_type=F32)
    dq, dk, dv = attention_backward(
        q_src, kv_src, cols, grad_attn, attn_f32, lse, seg_q, seg_row, head_dim
    )
    if by_heads:
        dqkv = to_rows_back(jnp.concatenate([dq, dk, dv], axis=2))
        dq, dk, dv = jnp.split(dqkv, 3, axis=2)
    else:
        dk, dv = (lax.psum_scatter(g, "blk", scatter_dimension=1, tiled=True) for g in (dk, dv))
    dq, dk, dv = (g.transpose(1, 0, 2) for g in (dq, dk, dv))
    grad_query_norm = rotate(dq.astype(F32), cos_table, -sin_table)
    grad_key_norm = rotate(dk.astype(F32), cos_table, -sin_table)
    grad_gain_query = jnp.sum(grad_query_norm * (query_raw * query_scale), axis=(0, 1))
    grad_gain_key = jnp.sum(grad_key_norm * (key_raw * key_scale), axis=(0, 1))
    grad_projected = jnp.concatenate(
        [
            norm_back(grad_query_norm * gain_query, query_raw, query_scale)
            .reshape(rows, local_width)
            .astype(BF16),
            norm_back(grad_key_norm * gain_key, key_raw, key_scale)
            .reshape(rows, local_width)
            .astype(BF16),
            dv.reshape(rows, local_width),
        ],
        axis=1,
    )
    grad_hidden_part = dot_nt(grad_projected, own_qkv)
    grad_hidden_one = sum_scatter(grad_hidden_part, ULY)
    grad_gain_attn = jnp.sum(grad_hidden_part * normed_one, axis=0)
    grad_inputs = grad_mid + norm_back(grad_hidden_one * gain_attn, inputs, rms_scale(inputs))

    grad_qkv_part = dot_tn(hidden_one, grad_projected).astype(BF16)
    grad_qkv_rows = lax.psum_scatter(grad_qkv_part, ROWS, scatter_dimension=0, tiled=True)
    grad_qkv_rows = swap(grad_qkv_rows.reshape(uly, shard_rows, 3 * local_width), ULY)
    grad_qkv = (
        grad_qkv_rows.reshape(uly, shard_rows, 3, local_width)
        .transpose(1, 2, 0, 3)
        .reshape(shard_rows, 3 * width)
        .astype(F32)
    )
    grad_out_rows = lax.psum_scatter(
        grad_out_part.reshape(local_width, width).astype(BF16), ROWS, scatter_dimension=0, tiled=True
    )
    grad_out = lax.ppermute(grad_out_rows, ALL, [(b, a) for a, b in to_rows]).astype(F32)
    small = jnp.concatenate([grad_gain_attn[:, None], grad_gain_ffn[:, None], grad_router_part], axis=1)
    small = lax.psum_scatter(small, ALL, scatter_dimension=0, tiled=True)
    grad_qk_gain = lax.psum(jnp.stack([grad_gain_query, grad_gain_key]), ALL)

    clip_gamma = TAU / jnp.maximum(head_max, TAU)
    factor = jnp.repeat(jnp.sqrt(clip_gamma), head_dim)
    column_scale = jnp.concatenate([factor, factor, jnp.ones((width,), F32)])
    clipped = w_qkv.astype(F32) * column_scale[None, :]
    return (
        output[None],
        grad_inputs[None],
        grad_qkv,
        grad_out,
        small[:, 0],
        small[:, 1],
        grad_qk_gain,
        small[:, 2:],
        grad_gate_up,
        grad_down,
        clipped,
    )


def per_device(
    tokens, segments, routes, w_qkv, w_out, attn_gain, ffn_gain, qk_gain, router, w_gate_up, w_down, cotangent
):
    own_tokens = tokens[0]
    own_grad = cotangent[0]
    count_tok, width = own_tokens.shape
    head_dim = qk_gain.shape[1]
    heads = width // head_dim
    batch, blk, uly = lax.axis_size("batch"), lax.axis_size("blk"), spread(ULY)
    total, group = batch * blk * uly, batch * blk
    local_experts = w_down.shape[0]
    if uly != 4 or heads != blk * uly or blk < 2 or batch != 2 or local_experts % 2:
        return per_device_general(
            tokens, segments, routes, w_qkv, w_out, attn_gain, ffn_gain, qk_gain, router, w_gate_up, w_down, cotangent
        )
    blk_at, uly_at = lax.axis_index("blk"), lax.axis_index(ULY)
    rows = count_tok * uly
    seg_row = segments[0]
    length = seg_row.shape[0]
    number = router.shape[1]
    shard_rows = w_qkv.shape[0]

    to_rows = [(u * group + g, g * uly + u) for g in range(group) for u in range(uly)]
    rows_here = lax.ppermute(w_out, ALL, to_rows)
    rows_there = lax.ppermute(w_out, ALL, [(a, (b + total // 2) % total) for a, b in to_rows])


    half = local_experts // 2

    def gather_experts(gate_up, down):
        return lax.all_gather(jnp.concatenate([gate_up, down], axis=2), PLANE, axis=0, tiled=False)

    weights_first = gather_experts(w_gate_up[:half], w_down[:half])
    extra = jnp.concatenate([attn_gain[None], ffn_gain[None], router.T], axis=0)
    kept = extra.shape[0]
    extra = jnp.pad(extra, ((0, -kept % 16), (0, -shard_rows % LANES)))
    by_head = w_qkv.reshape(shard_rows, 3, heads, head_dim).transpose(2, 0, 1, 3)
    own_qkv, extras, toks = startup(
        by_head.reshape(heads, shard_rows, 3 * head_dim), extra, own_tokens, 0
    )
    rows_here, rows_there, extras, later_gate_up, later_down = lax.optimization_barrier(
        (rows_here, rows_there, extras, w_gate_up[half:], w_down[half:])
    )
    weights_second = gather_experts(later_gate_up, later_down)
    is_first = lax.axis_index("batch") == 0
    pair = jnp.stack(
        [jnp.where(is_first, rows_here, rows_there), jnp.where(is_first, rows_there, rows_here)]
    )
    own_out = lax.all_to_all(
        jnp.broadcast_to(pair[None], (blk, *pair.shape)), "blk", split_axis=0, concat_axis=0, tiled=True
    )
    own_out = own_out.transpose(1, 0, 2, 3).reshape(blk, head_dim, width)
    own_qkv = own_qkv.reshape(width, 3 * head_dim)
    extras = extras.reshape(total, *extra.shape)[:, :kept, :shard_rows]
    extras = extras.transpose(1, 0, 2).reshape(kept, width)
    gain_attn = extras[0].astype(F32)
    gain_ffn = extras[1].astype(F32)
    router_t = extras[2:]

    gains = qk_gain.astype(F32)
    cos, sin = rope_rows(length, head_dim)
    hidden_one, qkv, raw = project(
        toks.reshape(length, width), gain_attn[None], own_qkv, cos, sin, gains
    )
    attn_low, attn_f32, lse, top = attention_forward(
        qkv[None], qkv[None], (0, 1, 2), seg_row, seg_row, head_dim
    )
    (attn_rows,) = exchange([(attn_low.reshape(blk, rows, head_dim), ("blk",), "swap")], 1)
    branch = jnp.einsum("htc,hcd->td", attn_rows, own_out, preferred_element_type=F32)
    branch, grad_blk, routes_blk = exchange(
        [
            (branch.astype(BF16).reshape(uly, count_tok, width), ULY, "pairsum"),
            (own_grad, ("blk",), "line"),
            (routes[0].T, ("blk",), "gather"),
        ],
        2,
    )
    inputs = own_tokens.astype(F32)
    mid = inputs + branch

    scale_two = rms_scale(mid)
    normed_two = mid * scale_two
    hidden_two = (normed_two * gain_ffn).astype(BF16)
    hidden_blk, hidden_t, grad_t = turn_gather(hidden_two, grad_blk, 3)
    tokens_blk = blk * count_tok
    hidden_blk = hidden_blk.reshape(tokens_blk, width)
    grad_blk = grad_blk.reshape(tokens_blk, width)
    probs_blk = jax.nn.softmax(dot_nt(hidden_blk, router_t), axis=1)
    names = jnp.arange(number, dtype=jnp.int32)
    chosen_blk = jnp.any(routes_blk[:, :, :, None] == names, axis=1).astype(F32)
    chosen_blk = chosen_blk.reshape(tokens_blk, number)
    gates = lax.dynamic_slice_in_dim(
        probs_blk * chosen_blk, blk_at * local_experts, local_experts, axis=1
    )
    shared = (hidden_blk, hidden_t, grad_blk, grad_t)
    out_part, dx_part, dg_first, grads_first = experts(
        *shared, gates[:, :half], [(weights_first, 0, half)]
    )
    sums_first = lax.psum_scatter(grads_first, PLANE, scatter_dimension=0, tiled=False)
    out_part, dx_part, dg_others, grads_others = experts(
        *shared, gates[:, half:], [(weights_second, 0, half)], before=(out_part, dx_part)
    )
    sums_others = lax.psum_scatter(grads_others, PLANE, scatter_dimension=0, tiled=False)
    finished = finish_experts(sums_first, 0, local_experts)
    grad_gate_up, grad_down = finish_experts(sums_others, half, local_experts, before=finished)
    dg_part = jnp.concatenate([dg_first, dg_others], axis=0)
    dg_part = dg_part.reshape(local_experts, blk, count_tok)
    dx_parts, dg_parts = exchange(
        [
            (dx_part.reshape(blk, count_tok, width), ("blk",), "swap"),
            (dg_part.transpose(1, 0, 2), ("blk",), "swap"),
        ],
        4,
    )
    out_part = out_part.reshape(blk, count_tok, width)
    out_part, dx_parts = lax.optimization_barrier((out_part, dx_parts))
    out_parts = lax.all_to_all(out_part, "blk", split_axis=0, concat_axis=0, tiled=True)
    output = (mid + jnp.sum(out_parts.astype(F32), axis=0)).astype(BF16)
    router_probs = lax.dynamic_slice_in_dim(probs_blk, blk_at * count_tok, count_tok)
    chosen = lax.dynamic_slice_in_dim(chosen_blk, blk_at * count_tok, count_tok)
    grad_probs = chosen * dg_parts.reshape(number, count_tok).T
    grad_logits = (
        router_probs * (grad_probs - jnp.sum(router_probs * grad_probs, axis=1, keepdims=True))
    ).astype(BF16)
    grad_hidden_two = jnp.sum(dx_parts.astype(F32), axis=0) + dot_nn(grad_logits, router_t)
    grad_router_t = dot_tn(grad_logits, hidden_two)
    grad_gain_ffn = jnp.sum(grad_hidden_two * normed_two, axis=0)
    grad_mid = own_grad.astype(F32) + norm_back(grad_hidden_two * gain_ffn, mid, scale_two)

    (branch_grad,) = exchange([(grad_mid.astype(BF16), ULY, "relay")], 5)
    branch_grad, sent_qkv = lax.optimization_barrier((branch_grad, own_qkv))
    far_qkv = lax.ppermute(sent_qkv, "y", [(0, 1), (1, 0)])
    branch_grad = branch_grad.reshape(rows, width)
    grad_attn = jnp.einsum("td,hcd->htc", branch_grad, own_out, preferred_element_type=F32).astype(BF16)
    grad_out_part = jnp.einsum("htc,td->hcd", attn_rows, branch_grad, preferred_element_type=F32)
    grad_out_part = grad_out_part.astype(BF16).reshape(batch, blk, shard_rows, width)
    batch_at = lax.axis_index("batch")
    grad_attn, got_out_part = exchange(
        [
            (grad_attn, ("blk",), "swap"),
            (
                lax.dynamic_index_in_dim(grad_out_part, 1 - batch_at, 0, keepdims=False),
                ("batch",),
                "trade",
            ),
        ],
        6,
        after=[out_parts],
    )
    grad_out_part = lax.dynamic_index_in_dim(grad_out_part, batch_at, 0, keepdims=False) + got_out_part
    grad_projected, grad_gains = project_back(
        qkv, grad_attn.reshape(length, head_dim), attn_f32, lse, seg_row, raw, cos, sin, gains
    )
    grad_qkv_part = dot_tn(hidden_one, grad_projected).astype(BF16)
    by_batch = grad_qkv_part.reshape(batch, width // batch, 3 * head_dim)
    projected_blk, got_qkv_part, near_qkv, cross_qkv, grad_out_parts = exchange(
        [
            (grad_projected.reshape(blk, uly, count_tok, 3 * head_dim), ULY, "swap1"),
            (
                lax.dynamic_index_in_dim(by_batch, 1 - batch_at, 0, keepdims=False),
                ("batch",),
                "trade",
            ),
            (own_qkv, ("core",), "trade"),
            (far_qkv, ("core",), "trade"),
            (grad_out_part, ("blk",), "swap"),
        ],
        7,
    )
    grad_out = lax.ppermute(
        jnp.sum(grad_out_parts.astype(F32), axis=0).astype(BF16), ALL, [(b, a) for a, b in to_rows]
    ).astype(F32)
    grad_qkv_part = lax.dynamic_index_in_dim(by_batch, batch_at, 0, keepdims=False) + got_qkv_part

    grad_hidden_part, grad_gain_attn = hidden_back(
        projected_blk.reshape(uly, tokens_blk, 3 * head_dim),
        own_qkv,
        near_qkv,
        far_qkv,
        cross_qkv,
        hidden_one.reshape(blk, uly, count_tok, width),
    )
    grad_gain_attn = grad_gain_attn[0] / gain_attn

    small = jnp.concatenate([grad_gain_attn[None], grad_gain_ffn[None], grad_router_t], axis=0)
    beside = LANES // shard_rows
    small = jnp.pad(small, ((0, -kept % beside), (0, 0))).reshape(-1, beside, total, shard_rows)
    small = small.transpose(2, 0, 1, 3).reshape(total, -1, LANES)
    packed_rows = small.shape[1]
    head_row = jnp.where(
        jnp.arange(LANES) == uly_at * blk + blk_at, jnp.max(top) * head_dim**-0.5, NEG
    )
    to_all = jnp.concatenate([grad_gains, head_row[None]], axis=0)
    small = jnp.concatenate([small, jnp.broadcast_to(to_all[None], (total, 3, LANES))], axis=1)
    small = jnp.pad(small, ((0, 0), (0, -small.shape[1] % 8), (0, 0)))
    grad_hidden_parts, small, grad_qkv_parts = exchange(
        [
            (grad_hidden_part, ("blk",), "swap"),
            (small, ALL, "swap"),
            (grad_qkv_part.reshape(total // batch, shard_rows, 3 * head_dim), ("blk", *ULY), "swap"),
        ],
        8,
    )
    grad_qkv = merge_heads(grad_qkv_parts.reshape(blk, uly, shard_rows, 3 * head_dim))
    grad_hidden_one = jnp.sum(grad_hidden_parts.astype(F32), axis=0)
    grad_inputs = grad_mid + norm_back(grad_hidden_one * gain_attn, inputs, rms_scale(inputs))
    sums = jnp.sum(small, axis=0)
    sums, grad_gains = sums[:packed_rows], sums[packed_rows : packed_rows + 2]
    sums = sums.reshape(packed_rows * beside, shard_rows)[:kept]
    head_max = jnp.max(small[:, packed_rows + 2, :heads], axis=0)
    factor = jnp.repeat(jnp.sqrt(TAU / jnp.maximum(head_max, TAU)), head_dim)
    column_scale = jnp.concatenate([factor, factor, jnp.ones((width,), F32)])
    clipped = w_qkv.astype(F32) * column_scale[None, :]
    return (
        output[None],
        grad_inputs[None],
        grad_qkv,
        grad_out,
        sums[0],
        sums[1],
        grad_gains,
        sums[2:].T,
        grad_gate_up,
        grad_down,
        clipped,
    )


def solution(mesh):
    in_specs = (
        P("batch", ("blk", *ULY), None),
        P("batch", None),
        P("batch", ("blk", *ULY), None),
        P(ALL, None),
        P(ALL, None),
        P(ALL),
        P(ALL),
        P(),
        P(ALL, None),
        P("blk", PLANE, None),
        P("blk", PLANE, None),
        P("batch", ("blk", *ULY), None),
    )
    out_specs = (
        P("batch", ("blk", *ULY), None),
        P("batch", ("blk", *ULY), None),
        P(ALL, None),
        P(ALL, None),
        P(ALL),
        P(ALL),
        P(),
        P(ALL, None),
        P("blk", PLANE, None),
        P("blk", PLANE, None),
        P(ALL, None),
    )
    cores = 2 - mesh.shape["uly"] % 2
    mesh = Mesh(
        mesh.devices.reshape(*(mesh.shape[axis] for axis in ROWS), mesh.shape["uly"] // cores, cores), ALL
    )
    return jax.shard_map(
        per_device, mesh=mesh, in_specs=in_specs, out_specs=out_specs, check_vma=False
    )
```

profile of v0, /device:TPU:0, one launch (start us, length us, event | category | flops | bytes accessed | tf_op | source)
XLA Modules:
  0.0 698.0 jit_solution(7271750299178265276)
XLA Ops:
  7.2 2.8 fusion.26
  12.4 3.0 collective-permute-start.1
  15.4 3.6 collective-permute-start
  21.8 84.7 %startup.1 = (bf16[2,16,64,384]{3,2,1,0:T(8,128)(2,1)}, bf16[2,16,32,128]{3,2,1,0:T(8,128)(2,1)}, bf16[4,4,128,2048]{3,2,1,0:T(8,128)(2,1)}) custom-call(bf16[16,64,384]{2,1,0:T(8,128)(2,1)} %reshape.355.head_ref, bf16[32,128]{1,0:T(8,128)(2,1)} %fusion.23.extra_ref, bf16[128,2048]{1,0:T(8,128)(2,1)} %bitcast.130), custom_call_target="tpu_custom_call" | custom-call | tf_op jit(solution)/shard_map/startup/pallas_call | solution.py:1174
  106.5 3.4 pad_maximum_fusion
  112.7 5.9 all-to-all-start
  124.4 13.1 %project.1 = (bf16[2048,2048]{1,0:T(8,128)(2,1)}, bf16[2048,384]{1,0:T(8,128)(2,1)}, f32[2048,256]{1,0:T(8,128)}) custom-call(bf16[2048,2048]{1,0:T(8,128)(2,1)} %bitcast.132, f32[1,2048]{1,0:T(1,128)} %reshape.381.gain_ref, bf16[2048,384]{1,0:T(8,128)(2,1)} %bitcast.122, f32[2048,128]{1,0:T(8,128)} %bitcast.136, ...), custom_call_target="tpu_custom_call" | custom-call | tf_op jit(solution)/shard_map/project/pallas_call | solution.py:442
  137.4 9.9 %attend.1 = (bf16[1,2048,128]{2,1,0:T(8,128)(2,1)}, f32[1,2048,128]{2,1,0:T(8,128)}, f32[1,1,2048]{2,1,0:T(1,128)}, f32[1,1,2048]{2,1,0:T(1,128)}) custom-call(bf16[1,2048,384]{2,1,0:T(8,128)(2,1)} %bitcast.186, bf16[1,2048,384]{2,1,0:T(8,128)(2,1)} %bitcast.187, bf16[1,2048,384]{2,1,0:T(8,128)(2,1)} %bitcast.188, s32[1,2048]{1,0:T(1,128)} %sq_ref.3, ...), custom_call_target="tpu_custom_call" | custom-call | flops 2147483648 | bytes 4194304 | tf_op jit(solution)/shard_map/attend/pallas_call | solution.py:179
  147.3 29.6 %exchange.7 = bf16[4,512,128]{2,1,0:T(8,128)(2,1)} custom-call(bf16[4,512,128]{2,1,0:T(8,128)(2,1)} %bitcast.162), custom_call_target="tpu_custom_call" | custom-call | tf_op jit(solution)/shard_map/exchange/pallas_call | solution.py:872
  178.0 2.6 bitcast_convert_fusion
  180.6 42.2 %exchange.8 = (f32[128,2048]{1,0:T(8,128)}, bf16[4,128,2048]{2,1,0:T(8,128)(2,1)}, s32[4,8,128]{2,1,0:T(8,128)}) custom-call(bf16[4,128,2048]{2,1,0:T(8,128)(2,1)} %bitcast.146, bf16[128,2048]{1,0:T(8,128)(2,1)} %bitcast.134, s32[8,128]{1,0:T(8,128)} %bitcast.176), custom_call_target="tpu_custom_call" | custom-call | tf_op jit(solution)/shard_map/exchange/pallas_call | solution.py:872
  226.3 36.6 %turn_gather.1 = (bf16[4,128,2048]{2,1,0:T(8,128)(2,1)}, bf16[2048,512]{1,0:T(8,128)(2,1)}, bf16[2048,512]{1,0:T(8,128)(2,1)}) custom-call(bf16[128,2048]{1,0:T(8,128)(2,1)} %multiply_convert_fusion.refs_0_, bf16[4,128,2048]{2,1,0:T(8,128)(2,1)} %get-tuple-element.81.refs_1_), custom_call_target="tpu_custom_call" | custom-call | tf_op jit(solution)/shard_map/turn_gather/pallas_call | solution.py:988
  262.9 2.3 fusion.28
  266.8 51.4 %experts.2 = (bf16[512,2048]{1,0:T(8,128)(2,1)}, bf16[512,2048]{1,0:T(8,128)(2,1)}, f32[2,512,1]{2,1,0:T(8,128)}, bf16[8,3,2,256,1024]{4,3,2,1,0:T(8,128)(2,1)}) custom-call(bf16[512,2048]{1,0:T(8,128)(2,1)} %bitcast.148, bf16[2048,512]{1,0:T(8,128)(2,1)} %get-tuple-element.83.refs_1_, bf16[512,2048]{1,0:T(8,128)(2,1)} %bitcast.144, ...), custom_call_target="tpu_custom_call" | custom-call | flops 38654705664 | bytes 50331648 | tf_op jit(solution)/shard_map/experts/pallas_call | solution.py:340
  318.6 52.8 %experts.3 = (bf16[512,2048]{1,0:T(8,128)(2,1)}, bf16[512,2048]{1,0:T(8,128)(2,1)}, f32[2,512,1]{2,1,0:T(8,128)}, bf16[8,3,2,256,1024]{4,3,2,1,0:T(8,128)(2,1)}) custom-call(bf16[512,2048]{1,0:T(8,128)(2,1)} %bitcast.149, bf16[2048,512]{1,0:T(8,128)(2,1)} %get-tuple-element.83.refs_1_, bf16[512,2048]{1,0:T(8,128)(2,1)} %bitcast.145, ...), custom_call_target="tpu_custom_call" | custom-call | flops 38654705664 | bytes 50331648 | tf_op jit(solution)/shard_map/experts/pallas_call | solution.py:340
  374.4 47.0 %exchange.9 = (bf16[4,128,2048]{2,1,0:T(8,128)(2,1)}, f32[4,4,128]{2,1,0:T(4,128)}) custom-call(bf16[4,128,2048]{2,1,0:T(8,128)(2,1)} %bitcast.153, f32[4,4,128]{2,1,0:T(4,128)} %maximum_bitcast_fusion.refs_1_), custom_call_target="tpu_custom_call" | custom-call | tf_op jit(solution)/shard_map/exchange/pallas_call | solution.py:872
  421.4 3.9 all-to-all-start.1
  433.7 30.5 %exchange.10 = bf16[4,128,2048]{2,1,0:T(8,128)(2,1)} custom-call(bf16[128,2048]{1,0:T(8,128)(2,1)} %fusion.24.refs_0_), custom_call_target="tpu_custom_call" | custom-call | tf_op jit(solution)/shard_map/exchange/pallas_call | solution.py:872
  464.2 2.3 collective-permute-start.2
  467.8 3.2 convolution_convert_fusion
  473.7 2.2 fusion.2.refs_0_
  477.2 27.8 %exchange.11 = (bf16[4,512,128]{2,1,0:T(8,128)(2,1)}, bf16[4,64,2048]{2,1,0:T(8,128)(2,1)}) custom-call(bf16[4,512,128]{2,1,0:T(8,128)(2,1)} %fusion.2.refs_0_, bf16[4,64,2048]{2,1,0:T(8,128)(2,1)} %dynamic-slice_bitcast_fusion.refs_1_, bf16[4,128,2048]{2,1,0:T(8,128)(2,1)} %copy-done), custom_call_target="tpu_custom_call" | custom-call | tf_op jit(solution)/shard_map/exchange/pallas_call | solution.py:872
  505.0 20.8 %project_back.1 = (bf16[2048,384]{1,0:T(8,128)(2,1)}, f32[2,128]{1,0:T(2,128)}) custom-call(bf16[2048,384]{1,0:T(8,128)(2,1)} %get-tuple-element.76.q_ref.k_ref.v_ref, bf16[2048,384]{1,0:T(8,128)(2,1)} %get-tuple-element.76.q_ref.k_ref.v_ref, bf16[2048,384]{1,0:T(8,128)(2,1)} %get-tuple-element.76.q_ref.k_ref.v_ref, bf16[2048,128]{1,0:T(8,128)(2,1)} %bitcast.189, ...), custom_call_target="tpu_custom_call" | custom-call | flops 5368709120 | bytes 10485760 | tf_op jit(solution)/shard_map/project_back/pallas_call | solution.py:526
  525.9 10.8 %convolution_convert_fusion.1 = bf16[2048,384]{1,0:T(8,128)(2,1)S(1)} fusion(bf16[2048,2048]{1,0:T(8,128)(2,1)} %get-tuple-element.104, bf16[2048,384]{1,0:T(8,128)(2,1)} %get-tuple-element.103), kind=kOutput, calls=%fused_computation.7 | convolution fusion | flops 3222011904 | bytes 11534336 | tf_op jit(solution)/shard_map/dot_general | solution.py:82
  539.6 28.8 %exchange.12 = (bf16[4,4,128,384]{3,2,1,0:T(8,128)(2,1)}, bf16[1024,384]{1,0:T(8,128)(2,1)}, bf16[2048,384]{1,0:T(8,128)(2,1)}, bf16[2048,384]{1,0:T(8,128)(2,1)}, bf16[4,64,2048]{2,1,0:T(8,128)(2,1)}) custom-call(bf16[4,4,128,384]{3,2,1,0:T(8,128)(2,1)} %bitcast.156, bf16[1024,384]{1,0:T(8,128)(2,1)} %dynamic-slice_bitcast_fusion.1.refs_1_, ...), custom_call_target="tpu_custom_call" | custom-call | tf_op jit(solution)/shard_map/exchange/pallas_call | solution.py:872
  568.3 9.2 %hidden_back.1 = (bf16[4,128,2048]{2,1,0:T(8,128)(2,1)}, f32[1,2048]{1,0:T(1,128)}) custom-call(bf16[4,512,384]{2,1,0:T(8,128)(2,1)} %bitcast.157, bf16[2048,384]{1,0:T(8,128)(2,1)} %bitcast.125, bf16[2048,384]{1,0:T(8,128)(2,1)} %get-tuple-element.108.near_ref, bf16[2048,384]{1,0:T(8,128)(2,1)} %collective-permute-done.2.refs_3_.far_ref, ...), custom_call_target="tpu_custom_call" | custom-call | tf_op jit(solution)/shard_map/hidden_back/pallas_call | solution.py:590
  584.7 72.6 %exchange.13 = (bf16[4,128,2048]{2,1,0:T(8,128)(2,1)}, f32[32,16,128]{2,1,0:T(8,128)}, bf16[16,64,384]{2,1,0:T(8,128)(2,1)}) custom-call(bf16[4,128,2048]{2,1,0:T(8,128)(2,1)} %get-tuple-element.110.refs_0_, f32[32,16,128]{2,1,0:T(8,128)} %select_maximum_fusion.refs_1_, bf16[16,64,384]{2,1,0:T(8,128)(2,1)} %bitcast.141), custom_call_target="tpu_custom_call" | custom-call | tf_op jit(solution)/shard_map/exchange/pallas_call | solution.py:872
  658.4 2.6 convert_reduce_fusion
  665.7 2.5 merge_heads.1
  670.6 5.0 finish_experts.2
  675.6 10.4 %reduce-scatter.3.cloned.1.call-done = bf16[1,3,2,256,1024]{4,3,2,1,0:T(8,128)(2,1)} async-done(((bf16[8,3,2,256,1024]{4,3,2,1,0:T(8,128)(2,1)}), bf16[1,3,2,256,1024]{4,3,2,1,0:T(8,128)(2,1)}) %reduce-scatter.3.cloned.1.call-update) | async-done | bytes 3145744 | tf_op jit(solution)/shard_map/reduce_scatter | solution.py:1523
  686.0 5.0 finish_experts.3
  (176 shorter events, 53.9 us)
Async XLA Ops:
  7.2 259.7 %all-gather.7.cloned.1.call-start = ((), (), s32[]{:S(2)}) async-start(), calls=%async_computation.7 | async-start | bytes 28311552 | tf_op jit(solution)/shard_map/all_gather | solution.py:1451
  7.2 2.9 copy-start.11
  12.4 6.7 copy-start.12
  12.4 306.2 %all-gather.5.cloned.1.call-start = ((), (), s32[]{:S(2)}) async-start(), calls=%async_computation.6 | async-start | bytes 28311552 | tf_op jit(solution)/shard_map/all_gather | solution.py:1451
  12.4 94.0 %collective-permute-start.1 = (bf16[64,2048]{1,0:T(8,128)(2,1)}, bf16[64,2048]{1,0:T(8,128)(2,1)S(1)}, u32[]{:S(2)}, u32[]{:S(2)}) collective-permute-start(bf16[64,2048]{1,0:T(8,128)(2,1)} %param.16), channel_id=1, source_target_pairs={{0,16},{8,17},{16,18},{24,19},{1,20},{9,21},{17,22},{25,23},{2,24}... | collective-permute-start | bytes 786440 | tf_op jit(solution)/shard_map/ppermute | solution.py:1445
  15.4 91.0 %collective-permute-start = (bf16[64,2048]{1,0:T(8,128)(2,1)}, bf16[64,2048]{1,0:T(8,128)(2,1)}, u32[]{:S(2)}, u32[]{:S(2)}) collective-permute-start(bf16[64,2048]{1,0:T(8,128)(2,1)} %param.16), channel_id=1, source_target_pairs={{0,0},{8,1},{16,2},{24,3},{1,4},{9,5},{17,6},{25,7},{2,8},{10,9},{... | collective-permute-start | bytes 786440 | tf_op jit(solution)/shard_map/ppermute | solution.py:1444
  112.7 6.0 copy-start.37
  112.7 7.0 %copy-start.26 = (s32[1,2048]{1,0:T(1,128)S(1)}, s32[1,2048]{1,0:T(1,128)}, u32[]{:S(2)}) copy-start(s32[1,2048]{1,0:T(1,128)} %sq_ref.3) | copy-start | bytes 24580
  112.7 64.2 %all-to-all-start = ((bf16[4,2,64,2048]{3,2,1,0:T(8,128)(2,1)}), bf16[4,2,64,2048]{3,2,1,0:T(8,128)(2,1)S(1)}, u32[]{:S(2)}, u32[]{:S(2)}) async-start(bf16[4,2,64,2048]{3,2,1,0:T(8,128)(2,1)} %broadcast_in_dim.41), calls=%async_computation | async-start | bytes 4194304 | tf_op jit(solution)/shard_map/all_to_all | solution.py:1469
  118.6 551.9 %reduce-scatter.5.cloned.1.call-start = ((), (), s32[]{:S(2)}) async-start(), calls=%async_computation.5 | async-start | bytes 28311552 | tf_op jit(solution)/shard_map/reduce_scatter | solution.py:1519
  121.1 2.3 copy-start.24
  177.1 3.5 copy-start.15
  180.6 43.2 %copy-start.7 = (bf16[1,128,2048]{2,1,0:T(8,128)(2,1)S(1)}, bf16[1,128,2048]{2,1,0:T(8,128)(2,1)}, u32[]{:S(2)}) copy-start(bf16[1,128,2048]{2,1,0:T(8,128)(2,1)} %param.12) | copy-start | bytes 1572868
  223.7 42.0 %copy-start.20 = (pred[4,128,16]{2,1,0:T(8,128)(4,1)}, pred[4,128,16]{2,1,0:T(8,128)(4,1)S(1)}, u32[]{:S(2)}) copy-start(pred[4,128,16]{2,1,0:T(8,128)(4,1)S(1)} %copy.61) | copy-start | bytes 24580
  225.3 37.6 %copy-start.27 = (f32[128]{0:T(128)}, f32[128]{0:T(128)S(1)}, u32[]{:S(2)}) copy-start(f32[128]{0:T(128)S(1)} %add_rsqrt_fusion.1) | copy-start | bytes 1540
  318.3 367.7 %reduce-scatter.3.cloned.1.call-start = ((), (), s32[]{:S(2)}) async-start(), calls=%async_computation.4 | async-start | bytes 28311552 | tf_op jit(solution)/shard_map/reduce_scatter | solution.py:1523
  421.4 54.5 %all-to-all-start.1 = ((bf16[4,128,2048]{2,1,0:T(8,128)(2,1)}), bf16[4,128,2048]{2,1,0:T(8,128)(2,1)S(1)}, u32[]{:S(2)}, u32[]{:S(2)}) async-start(bf16[4,128,2048]{2,1,0:T(8,128)(2,1)} %bitcast.152), calls=%async_computation.1 | async-start | bytes 4194304 | tf_op jit(solution)/shard_map/all_to_all | solution.py:1537
  427.1 3.8 copy-start.28
  430.1 2.5 copy-start.9
  433.7 32.8 %copy-start.23 = (bf16[128,16]{1,0:T(8,128)(2,1)S(1)}, bf16[128,16]{1,0:T(8,128)(2,1)}, u32[]{:S(2)}) copy-start(bf16[128,16]{1,0:T(8,128)(2,1)} %copy-done.22) | copy-start | bytes 12292
  464.2 75.4 %collective-permute-start.2 = (bf16[2048,384]{1,0:T(8,128)(2,1)}, bf16[2048,384]{1,0:T(8,128)(2,1)}, u32[]{:S(2)}, u32[]{:S(2)}) collective-permute-start(bf16[2048,384]{1,0:T(8,128)(2,1)} %bitcast.123), channel_id=1, source_target_pairs={{0,2},{2,0},{1,3},{3,1},{4,6},{6,4},{5,7},{7,5},{8,10},{10,8},{9,1... | collective-permute-start | bytes 4718600 | tf_op jit(solution)/shard_map/ppermute | solution.py:1552
  467.8 4.8 copy-start.16
  471.0 2.7 copy-start.6
  525.9 11.8 %copy-start.5 = (bf16[4,128,2048]{2,1,0:T(8,128)(2,1)S(1)}, bf16[4,128,2048]{2,1,0:T(8,128)(2,1)}, u32[]{:S(2)}) copy-start(bf16[4,128,2048]{2,1,0:T(8,128)(2,1)} %copy-done.4) | copy-start | bytes 6291460
  568.3 9.2 %copy-start.25 = (f32[1,2048]{1,0:T(1,128)S(1)}, f32[1,2048]{1,0:T(1,128)}, u32[]{:S(2)}) copy-start(f32[1,2048]{1,0:T(1,128)} %reshape.381.gain_ref) | copy-start | bytes 24580
  577.6 4.2 copy-start.33
  577.6 4.2 copy-start.34
  580.4 88.3 %collective-permute-start.3 = (bf16[64,2048]{1,0:T(8,128)(2,1)S(1)}, bf16[64,2048]{1,0:T(8,128)(2,1)}, u32[]{:S(2)}, u32[]{:S(2)}) collective-permute-start(bf16[64,2048]{1,0:T(8,128)(2,1)S(1)} %reduce_sum.121), channel_id=1, source_target_pairs={{0,0},{1,8},{2,16},{3,24},{4,1},{5,9},{6,17},{7,25},{8,2},{9,10},{... | collective-permute-start | bytes 786440 | tf_op jit(solution)/shard_map/ppermute | solution.py:1590
  584.7 73.7 %copy-start.1 = (bf16[4,128,2048]{2,1,0:T(8,128)(2,1)S(1)}, bf16[4,128,2048]{2,1,0:T(8,128)(2,1)}, u32[]{:S(2)}) copy-start(bf16[4,128,2048]{2,1,0:T(8,128)(2,1)} %copy-done) | copy-start | bytes 6291460
  658.4 2.7 copy-start.8
  658.4 2.7 copy-start.32
  658.4 3.0 copy-start.13
  (16 other events, 24.7 us)
Sparse Core Ops, SparseCore 0:
  12.5 169.0 all-gather.6
  184.1 127.0 all-gather.4
  318.4 185.5 reduce-scatter.4
  507.5 178.4 reduce-scatter.2
where the time goes:
time: 709 us; the launch traced here: 698 us
  Pallas kernels  569 us (80%)
  other arithmetic  36.4 us (5%)
  local copies, waits for them, and re-layouts  22.9 us (3%)
  matrix products  22.8 us (3%)
  starting transfers between devices  20.4 us (3%)
  between operations  15.6 us (2%)
  waiting for transfers between devices  10.5 us (1%)
    pallas_call x7, Pallas kernels, exchange(): pl.pallas_call(kernel, in_specs=specs + [anywhere] * len(after), out_spec...  278 us
    pallas_call x2, Pallas kernels, experts(): pl.pallas_call(functools.partial(expert_kernel, bool(before), counts), gr...  104 us
    pallas_call x1, Pallas kernels, startup(): pl.pallas_call(startup_kernel, in_specs=[anywhere] * 3, out_specs=[anywhe...  84.7 us
    pallas_call x1, Pallas kernels, turn_gather(): pl.pallas_call(kernel, in_specs=[anywhere] * (2 + len(after)), out_specs=...  36.6 us
    pallas_call x1, Pallas kernels, project_back(): pl.pallas_call(functools.partial(project_back_kernel, head_dim ** (-0.5)...  20.8 us
  transfers between devices with their start and end apart: 10, of which 1 were waited for; matrix products, arithmetic and copies ran while one was open for 10% of the time, Pallas kernels for 81%

commit v1 on v0

--- a/solution.py
+++ b/solution.py
@@ -1009,8 +1009,8 @@
 
 
 def startup_kernel(
-    head_ref, extra_ref, tok_ref, heads_ref, extras_ref, toks_ref,
-    head_send, head_recv, extra_send, extra_recv, trade_send, trade_recv,
+    head_ref, extra_ref, tok_ref, rows_ref, heads_ref, extras_ref, toks_ref, pair_ref,
+    head_send, head_recv, extra_send, extra_recv, trade_send, trade_recv, rows_send, rows_recv,
     z_send, z_recv, ay_send, ay_recv, by_send, by_recv, c_send, c_recv, local,
 ):
     blk, uly = lax.axis_size("blk"), spread(ULY)
@@ -1093,6 +1093,23 @@
         ref = (heads_ref, extras_ref)[which].at[b]
         return send(ref, ref, trade_send.at[which], trade_recv.at[which], {"batch": 1 - b})
 
+    batch = lax.axis_size("batch")
+    shards = batch * blk
+    keeper, number = me // shards, lax.rem(me, shards)
+
+    def rows_to(target):
+        to = (target * blk + lax.rem(number, blk)) * uly + keeper
+        slot = number // blk
+        copy = send(rows_ref, pair_ref.at[slot], rows_send.at[target], rows_recv.at[slot], place(ALL, to))
+        return to != me, copy
+
+    def rows_from(slot):
+        sender = u * shards + slot * blk + z
+        copy = send(rows_ref, pair_ref.at[slot], rows_send.at[slot], rows_recv.at[slot], place(ALL, sender))
+        return sender != me, copy
+
+    rows_own = pltpu.make_async_copy(rows_ref, pair_ref.at[number // blk], local.at[3])
+    keeps_own = (keeper == u) & (lax.rem(number, blk) == z)
     own = [
         pltpu.make_async_copy(tok_ref, toks_ref.at[z, u], local.at[0]),
         pltpu.make_async_copy(head_ref.at[u * blk + z], heads_ref.at[b, mine], local.at[1]),
@@ -1115,6 +1132,9 @@
 
     for copy in own:
         copy.start()
+    for target in range(batch):
+        when(rows_to(target), lambda copy: copy.start())
+    pl.when(keeps_own)(lambda: rows_own.start())
     b_y().wait_recv()
     for up in ways:
         when(hop(2, up, 0), lambda copy: copy.start())
@@ -1154,6 +1174,10 @@
 
     trade(0).wait()
     trade(1).wait()
+    for target in range(batch):
+        when(rows_from(target), lambda copy: copy.wait_recv())
+        when(rows_to(target), lambda copy: copy.wait_send())
+    pl.when(keeps_own)(lambda: rows_own.wait())
     own[0].wait()
     b_y().wait_send()
     for hops in range(blk - 1):
@@ -1167,31 +1191,33 @@
                 to_near(step, other, part).wait_send()
 
 
-def startup(heads, extra, tok, collective_id):
+def startup(heads, extra, tok, out_rows, collective_id):
     batch, blk, uly = lax.axis_size("batch"), lax.axis_size("blk"), spread(ULY)
     anywhere = pl.BlockSpec(memory_space=pl.ANY)
     dma = pltpu.SemaphoreType.DMA
     return pl.pallas_call(
         startup_kernel,
-        in_specs=[anywhere] * 3,
-        out_specs=[anywhere] * 3,
+        in_specs=[anywhere] * 4,
+        out_specs=[anywhere] * 4,
         out_shape=[
             jax.ShapeDtypeStruct((batch, blk * uly, *heads.shape[1:]), BF16),
             jax.ShapeDtypeStruct((batch, blk * uly, *extra.shape), BF16),
             jax.ShapeDtypeStruct((blk, uly, *tok.shape), BF16),
+            jax.ShapeDtypeStruct((batch, *out_rows.shape), BF16),
         ],
         scratch_shapes=[
             *[dma((blk * uly,))] * 4,
             *[dma((2,))] * 2,
+            *[dma((batch,))] * 2,
             *[dma((6 * blk,))] * 2,
             *[dma((blk,))] * 2,
             *[dma((1,))] * 2,
             *[dma((4 * blk,))] * 2,
-            dma((3,)),
+            dma((4,)),
         ],
         compiler_params=pltpu.CompilerParams(collective_id=collective_id, has_side_effects=True),
         name="startup",
-    )(heads, extra, tok)
+    )(heads, extra, tok, out_rows)
 
 
 def per_device_general(
@@ -1441,8 +1467,6 @@
     shard_rows = w_qkv.shape[0]
 
     to_rows = [(u * group + g, g * uly + u) for g in range(group) for u in range(uly)]
-    rows_here = lax.ppermute(w_out, ALL, to_rows)
-    rows_there = lax.ppermute(w_out, ALL, [(a, (b + total // 2) % total) for a, b in to_rows])
 
 
     half = local_experts // 2
@@ -1455,17 +1479,11 @@
     kept = extra.shape[0]
     extra = jnp.pad(extra, ((0, -kept % 16), (0, -shard_rows % LANES)))
     by_head = w_qkv.reshape(shard_rows, 3, heads, head_dim).transpose(2, 0, 1, 3)
-    own_qkv, extras, toks = startup(
-        by_head.reshape(heads, shard_rows, 3 * head_dim), extra, own_tokens, 0
-    )
-    rows_here, rows_there, extras, later_gate_up, later_down = lax.optimization_barrier(
-        (rows_here, rows_there, extras, w_gate_up[half:], w_down[half:])
-    )
+    own_qkv, extras, toks, pair = startup(
+        by_head.reshape(heads, shard_rows, 3 * head_dim), extra, own_tokens, w_out, 0
+    )
+    extras, later_gate_up, later_down = lax.optimization_barrier((extras, w_gate_up[half:], w_down[half:]))
     weights_second = gather_experts(later_gate_up, later_down)
-    is_first = lax.axis_index("batch") == 0
-    pair = jnp.stack(
-        [jnp.where(is_first, rows_here, rows_there), jnp.where(is_first, rows_there, rows_here)]
-    )
     own_out = lax.all_to_all(
         jnp.broadcast_to(pair[None], (blk, *pair.shape)), "blk", split_axis=0, concat_axis=0, tiled=True
     )
@@ -1555,25 +1573,16 @@
     grad_out_part = jnp.einsum("htc,td->hcd", attn_rows, branch_grad, preferred_element_type=F32)
     grad_out_part = grad_out_part.astype(BF16).reshape(batch, blk, shard_rows, width)
     batch_at = lax.axis_index("batch")
-    grad_attn, got_out_part = exchange(
-        [
-            (grad_attn, ("blk",), "swap"),
-            (
-                lax.dynamic_index_in_dim(grad_out_part, 1 - batch_at, 0, keepdims=False),
-                ("batch",),
-                "trade",
-            ),
-        ],
-        6,
-        after=[out_parts],
-    )
-    grad_out_part = lax.dynamic_index_in_dim(grad_out_part, batch_at, 0, keepdims=False) + got_out_part
+    (grad_attn,) = exchange([(grad_attn, ("blk",), "swap")], 6, after=[out_parts])
+    grad_out_part, grad_attn = lax.optimization_barrier((grad_out_part, grad_attn))
+    grad_out_parts = lax.all_to_all(grad_out_part, "blk", split_axis=1, concat_axis=0, tiled=False)
+    grad_out_part = jnp.sum(grad_out_parts.astype(F32), axis=0).astype(BF16)
     grad_projected, grad_gains = project_back(
         qkv, grad_attn.reshape(length, head_dim), attn_f32, lse, seg_row, raw, cos, sin, gains
     )
     grad_qkv_part = dot_tn(hidden_one, grad_projected).astype(BF16)
     by_batch = grad_qkv_part.reshape(batch, width // batch, 3 * head_dim)
-    projected_blk, got_qkv_part, near_qkv, cross_qkv, grad_out_parts = exchange(
+    projected_blk, got_qkv_part, near_qkv, cross_qkv, got_out_part = exchange(
         [
             (grad_projected.reshape(blk, uly, count_tok, 3 * head_dim), ULY, "swap1"),
             (
@@ -1583,13 +1592,16 @@
             ),
             (own_qkv, ("core",), "trade"),
             (far_qkv, ("core",), "trade"),
-            (grad_out_part, ("blk",), "swap"),
+            (
+                lax.dynamic_index_in_dim(grad_out_part, 1 - batch_at, 0, keepdims=False),
+                ("batch",),
+                "trade",
+            ),
         ],
         7,
     )
-    grad_out = lax.ppermute(
-        jnp.sum(grad_out_parts.astype(F32), axis=0).astype(BF16), ALL, [(b, a) for a, b in to_rows]
-    ).astype(F32)
+    grad_out_part = lax.dynamic_index_in_dim(grad_out_part, batch_at, 0, keepdims=False) + got_out_part
+    grad_out = lax.ppermute(grad_out_part, ALL, [(b, a) for a, b in to_rows]).astype(F32)
     grad_qkv_part = lax.dynamic_index_in_dim(by_batch, batch_at, 0, keepdims=False) + got_qkv_part
 
     grad_hidden_part, grad_gain_attn = hidden_back(

time: 709 us -> 735 us (1.037)
  Pallas kernels: 569 us -> 588 us
    pallas_call x1, Pallas kernels: 84.7 us -> 97.4 us  [startup(): pl.pallas_call(startup_kernel, in_specs=[anywhere] * 4, out_specs=[anywhe...]
    reduce_scatter x1, waiting for transfers between devices: 10.4 us -> 0.01 us  [per_device(): lax.psum_scatter(grads_others, PLANE, scatter_dimension=0, tiled=False)]
    all_to_all x0 -> x1, waiting for transfers between devices: none -> 8.25 us  [per_device(): lax.all_to_all(grad_out_part, 'blk', split_axis=1, concat_axis=0, tiled=F...]
  transfers between devices with their start and end apart: 10 -> 9, of which waited for: 1 -> 2; matrix products, arithmetic and copies ran while one was open for 10% -> 10% of each run, Pallas kernels for 81% -> 81%
where the time goes in v1:
time: 735 us; the launch traced here: 721 us
  Pallas kernels  588 us (80%)
  other arithmetic  32.6 us (4%)
  local copies, waits for them, and re-layouts  30.1 us (4%)
  matrix products  21.2 us (3%)
  starting transfers between devices  18.2 us (2%)
  waiting for transfers between devices  15.7 us (2%)
  between operations  15.3 us (2%)
    pallas_call x7, Pallas kernels, exchange(): pl.pallas_call(kernel, in_specs=specs + [anywhere] * len(after), out_spec...  283 us
    pallas_call x2, Pallas kernels, experts(): pl.pallas_call(functools.partial(expert_kernel, bool(before), counts), gr...  104 us
    pallas_call x1, Pallas kernels, startup(): pl.pallas_call(startup_kernel, in_specs=[anywhere] * 4, out_specs=[anywhe...  97.4 us
    pallas_call x1, Pallas kernels, turn_gather(): pl.pallas_call(kernel, in_specs=[anywhere] * (2 + len(after)), out_specs=...  36.9 us
    pallas_call x1, Pallas kernels, project_back(): pl.pallas_call(functools.partial(project_back_kernel, head_dim ** (-0.5)...  22.1 us
  transfers between devices with their start and end apart: 9, of which 2 were waited for; matrix products, arithmetic and copies ran while one was open for 10% of the time, Pallas kernels for 81%

profile of v1, /device:TPU:0, one launch (start us, length us, event | category | flops | bytes accessed | tf_op | source)
XLA Modules:
  0.0 720.7 jit_solution(7809820092659359554)
XLA Ops:
  7.2 2.8 fusion.26
  16.2 97.4 %startup.1 = (bf16[2,16,64,384]{3,2,1,0:T(8,128)(2,1)}, bf16[2,16,32,128]{3,2,1,0:T(8,128)(2,1)}, bf16[4,4,128,2048]{3,2,1,0:T(8,128)(2,1)}, bf16[2,64,2048]{2,1,0:T(8,128)(2,1)}) custom-call(bf16[16,64,384]{2,1,0:T(8,128)(2,1)} %reshape.356.head_ref, bf16[32,128]{1,0:T(8,128)(2,1)} %fusion.23.extra_ref, bf16[128,2048]{1,0:T(8,128)(2,1)} %bitcast.125, ...), custom_call_target="tpu_custom_call" | custom-call | tf_op jit(solution)/shard_map/startup/pallas_call | solution.py:1198
  118.2 3.7 all-to-all-start
  127.7 13.3 %project.1 = (bf16[2048,2048]{1,0:T(8,128)(2,1)}, bf16[2048,384]{1,0:T(8,128)(2,1)}, f32[2048,256]{1,0:T(8,128)}) custom-call(bf16[2048,2048]{1,0:T(8,128)(2,1)} %bitcast.129, f32[1,2048]{1,0:T(1,128)} %reshape.382.gain_ref, bf16[2048,384]{1,0:T(8,128)(2,1)} %bitcast.121, f32[2048,128]{1,0:T(8,128)} %bitcast.135, ...), custom_call_target="tpu_custom_call" | custom-call | tf_op jit(solution)/shard_map/project/pallas_call | solution.py:442
  141.0 9.8 %attend.1 = (bf16[1,2048,128]{2,1,0:T(8,128)(2,1)}, f32[1,2048,128]{2,1,0:T(8,128)}, f32[1,1,2048]{2,1,0:T(1,128)}, f32[1,1,2048]{2,1,0:T(1,128)}) custom-call(bf16[1,2048,384]{2,1,0:T(8,128)(2,1)} %bitcast.186, bf16[1,2048,384]{2,1,0:T(8,128)(2,1)} %bitcast.187, bf16[1,2048,384]{2,1,0:T(8,128)(2,1)} %bitcast.188, s32[1,2048]{1,0:T(1,128)} %sq_ref.3, ...), custom_call_target="tpu_custom_call" | custom-call | flops 2147483648 | bytes 4194304 | tf_op jit(solution)/shard_map/attend/pallas_call | solution.py:179
  150.9 29.2 %exchange.7 = bf16[4,512,128]{2,1,0:T(8,128)(2,1)} custom-call(bf16[4,512,128]{2,1,0:T(8,128)(2,1)} %bitcast.161), custom_call_target="tpu_custom_call" | custom-call | tf_op jit(solution)/shard_map/exchange/pallas_call | solution.py:872
  181.2 2.6 bitcast_convert_fusion
  183.8 43.3 %exchange.8 = (f32[128,2048]{1,0:T(8,128)}, bf16[4,128,2048]{2,1,0:T(8,128)(2,1)}, s32[4,8,128]{2,1,0:T(8,128)}) custom-call(bf16[4,128,2048]{2,1,0:T(8,128)(2,1)} %bitcast.145, bf16[128,2048]{1,0:T(8,128)(2,1)} %bitcast.133, s32[8,128]{1,0:T(8,128)} %bitcast.176), custom_call_target="tpu_custom_call" | custom-call | tf_op jit(solution)/shard_map/exchange/pallas_call | solution.py:872
  230.5 36.9 %turn_gather.1 = (bf16[4,128,2048]{2,1,0:T(8,128)(2,1)}, bf16[2048,512]{1,0:T(8,128)(2,1)}, bf16[2048,512]{1,0:T(8,128)(2,1)}) custom-call(bf16[128,2048]{1,0:T(8,128)(2,1)} %multiply_convert_fusion.refs_0_, bf16[4,128,2048]{2,1,0:T(8,128)(2,1)} %get-tuple-element.79.refs_1_), custom_call_target="tpu_custom_call" | custom-call | tf_op jit(solution)/shard_map/turn_gather/pallas_call | solution.py:988
  267.4 2.3 fusion.28
  271.4 51.4 %experts.2 = (bf16[512,2048]{1,0:T(8,128)(2,1)}, bf16[512,2048]{1,0:T(8,128)(2,1)}, f32[2,512,1]{2,1,0:T(8,128)}, bf16[8,3,2,256,1024]{4,3,2,1,0:T(8,128)(2,1)}) custom-call(bf16[512,2048]{1,0:T(8,128)(2,1)} %bitcast.147, bf16[2048,512]{1,0:T(8,128)(2,1)} %get-tuple-element.81.refs_1_, bf16[512,2048]{1,0:T(8,128)(2,1)} %bitcast.143, ...), custom_call_target="tpu_custom_call" | custom-call | flops 38654705664 | bytes 50331648 | tf_op jit(solution)/shard_map/experts/pallas_call | solution.py:340
  323.3 52.9 %experts.3 = (bf16[512,2048]{1,0:T(8,128)(2,1)}, bf16[512,2048]{1,0:T(8,128)(2,1)}, f32[2,512,1]{2,1,0:T(8,128)}, bf16[8,3,2,256,1024]{4,3,2,1,0:T(8,128)(2,1)}) custom-call(bf16[512,2048]{1,0:T(8,128)(2,1)} %bitcast.148, bf16[2048,512]{1,0:T(8,128)(2,1)} %get-tuple-element.81.refs_1_, bf16[512,2048]{1,0:T(8,128)(2,1)} %bitcast.144, ...), custom_call_target="tpu_custom_call" | custom-call | flops 38654705664 | bytes 50331648 | tf_op jit(solution)/shard_map/experts/pallas_call | solution.py:340
  378.2 46.7 %exchange.9 = (bf16[4,128,2048]{2,1,0:T(8,128)(2,1)}, f32[4,4,128]{2,1,0:T(4,128)}) custom-call(bf16[4,128,2048]{2,1,0:T(8,128)(2,1)} %bitcast.152, f32[4,4,128]{2,1,0:T(4,128)} %maximum_bitcast_fusion.refs_1_), custom_call_target="tpu_custom_call" | custom-call | tf_op jit(solution)/shard_map/exchange/pallas_call | solution.py:872
  424.9 3.6 all-to-all-start.1
  430.2 2.1 convert_reduce_fusion.1
  435.9 25.7 %exchange.10 = bf16[4,128,2048]{2,1,0:T(8,128)(2,1)} custom-call(bf16[128,2048]{1,0:T(8,128)(2,1)} %fusion.24.refs_0_), custom_call_target="tpu_custom_call" | custom-call | tf_op jit(solution)/shard_map/exchange/pallas_call | solution.py:872
  461.7 4.8 convolution_convert_fusion
  468.6 7.3 %all-to-all-done.1.refs_1_ = bf16[4,128,2048]{2,1,0:T(8,128)(2,1)S(1)} async-done(((bf16[4,128,2048]{2,1,0:T(8,128)(2,1)}), bf16[4,128,2048]{2,1,0:T(8,128)(2,1)S(1)}, u32[]{:S(2)}, u32[]{:S(2)}) %all-to-all-start.1) | async-done | bytes 2097184 | tf_op jit(solution)/shard_map/all_to_all | solution.py:1555
  477.2 12.5 %exchange.11 = bf16[4,512,128]{2,1,0:T(8,128)(2,1)} custom-call(bf16[4,512,128]{2,1,0:T(8,128)(2,1)} %fusion.2.refs_0_, bf16[4,128,2048]{2,1,0:T(8,128)(2,1)} %copy-done), custom_call_target="tpu_custom_call" | custom-call | tf_op jit(solution)/shard_map/exchange/pallas_call | solution.py:872
  489.7 3.1 copy.82
  492.9 4.8 all-to-all-start.2
  499.1 3.7 collective-permute-start
  503.0 22.1 %project_back.1 = (bf16[2048,384]{1,0:T(8,128)(2,1)}, f32[2,128]{1,0:T(2,128)}) custom-call(bf16[2048,384]{1,0:T(8,128)(2,1)} %get-tuple-element.75.q_ref.k_ref.v_ref, bf16[2048,384]{1,0:T(8,128)(2,1)} %get-tuple-element.75.q_ref.k_ref.v_ref, bf16[2048,384]{1,0:T(8,128)(2,1)} %get-tuple-element.75.q_ref.k_ref.v_ref, bf16[2048,128]{1,0:T(8,128)(2,1)} %bitcast.162, ...), custom_call_target="tpu_custom_call" | custom-call | flops 5368709120 | bytes 10485760 | tf_op jit(solution)/shard_map/project_back/pallas_call | solution.py:526
  525.9 8.7 %convolution_convert_fusion.1 = bf16[2048,384]{1,0:T(8,128)(2,1)S(1)} fusion(bf16[2048,2048]{1,0:T(8,128)(2,1)} %get-tuple-element.102, bf16[2048,384]{1,0:T(8,128)(2,1)} %get-tuple-element.101), kind=kOutput, calls=%fused_computation.7 | convolution fusion | flops 3222011904 | bytes 11534336 | tf_op jit(solution)/shard_map/dot_general | solution.py:82
  536.7 8.3 %all-to-all-done.2 = bf16[1,2,4,64,2048]{4,3,1,0,2:T(8,128)(2,1)} async-done(((bf16[1,2,4,64,2048]{4,3,1,0,2:T(8,128)(2,1)}), bf16[1,2,4,64,2048]{4,3,1,0,2:T(8,128)(2,1)}, u32[]{:S(2)}, u32[]{:S(2)}) %all-to-all-start.2) | async-done | bytes 2097184 | tf_op jit(solution)/shard_map/all_to_all | solution.py:1578
  547.7 52.8 %exchange.12 = (bf16[4,4,128,384]{3,2,1,0:T(8,128)(2,1)}, bf16[1024,384]{1,0:T(8,128)(2,1)}, bf16[2048,384]{1,0:T(8,128)(2,1)}, bf16[2048,384]{1,0:T(8,128)(2,1)}, bf16[64,2048]{1,0:T(8,128)(2,1)}) custom-call(bf16[4,4,128,384]{3,2,1,0:T(8,128)(2,1)} %bitcast.155, bf16[1024,384]{1,0:T(8,128)(2,1)} %dynamic-slice_bitcast_fusion.refs_1_, ...), custom_call_target="tpu_custom_call" | custom-call | tf_op jit(solution)/shard_map/exchange/pallas_call | solution.py:872
  600.5 8.8 %hidden_back.1 = (bf16[4,128,2048]{2,1,0:T(8,128)(2,1)}, f32[1,2048]{1,0:T(1,128)}) custom-call(bf16[4,512,384]{2,1,0:T(8,128)(2,1)} %bitcast.156, bf16[2048,384]{1,0:T(8,128)(2,1)} %bitcast.123, bf16[2048,384]{1,0:T(8,128)(2,1)} %get-tuple-element.106.near_ref, bf16[2048,384]{1,0:T(8,128)(2,1)} %collective-permute-done.refs_3_.far_ref, ...), custom_call_target="tpu_custom_call" | custom-call | tf_op jit(solution)/shard_map/hidden_back/pallas_call | solution.py:590
  619.4 72.4 %exchange.13 = (bf16[4,128,2048]{2,1,0:T(8,128)(2,1)}, f32[32,16,128]{2,1,0:T(8,128)}, bf16[16,64,384]{2,1,0:T(8,128)(2,1)}) custom-call(bf16[4,128,2048]{2,1,0:T(8,128)(2,1)} %get-tuple-element.108.refs_0_, f32[32,16,128]{2,1,0:T(8,128)} %select_maximum_fusion.refs_1_, bf16[16,64,384]{2,1,0:T(8,128)(2,1)} %bitcast.140), custom_call_target="tpu_custom_call" | custom-call | tf_op jit(solution)/shard_map/exchange/pallas_call | solution.py:872
  692.8 2.6 convert_reduce_fusion
  700.1 2.5 merge_heads.1
  703.9 5.0 finish_experts.2
  708.9 5.0 finish_experts.3
  (173 shorter events, 57.2 us)
Async XLA Ops:
  7.2 264.2 %all-gather.7.cloned.1.call-start = ((), (), s32[]{:S(2)}) async-start(), calls=%async_computation.8 | async-start | bytes 28311552 | tf_op jit(solution)/shard_map/all_gather | solution.py:1475
  7.2 2.9 copy-start.11
  12.4 310.9 %all-gather.5.cloned.1.call-start = ((), (), s32[]{:S(2)}) async-start(), calls=%async_computation.7 | async-start | bytes 28311552 | tf_op jit(solution)/shard_map/all_gather | solution.py:1475
  15.6 98.0 %copy-start.12 = (bf16[2,256,1024]{2,1,0:T(8,128)(2,1)S(1)}, bf16[2,256,1024]{2,1,0:T(8,128)(2,1)}, u32[]{:S(2)}) copy-start(bf16[2,256,1024]{2,1,0:T(8,128)(2,1)} %get-tuple-element.85) | copy-start | bytes 3145732
  118.2 3.8 copy-start.37
  118.2 4.9 copy-start.32
  118.2 6.2 copy-start.28
  118.2 62.0 %all-to-all-start = ((bf16[4,2,64,2048]{3,2,1,0:T(8,128)(2,1)}), bf16[4,2,64,2048]{3,2,1,0:T(8,128)(2,1)S(1)}, u32[]{:S(2)}, u32[]{:S(2)}) async-start(bf16[4,2,64,2048]{3,2,1,0:T(8,128)(2,1)} %broadcast_in_dim.43), calls=%async_computation | async-start | bytes 4194304 | tf_op jit(solution)/shard_map/all_to_all | solution.py:1487
  121.9 582.0 %reduce-scatter.5.cloned.1.call-start = ((), (), s32[]{:S(2)}) async-start(), calls=%async_computation.6 | async-start | bytes 28311552 | tf_op jit(solution)/shard_map/reduce_scatter | solution.py:1537
  124.6 3.1 copy-start.29
  180.3 3.5 copy-start.16
  183.7 44.2 %copy-start.5 = (bf16[1,128,2048]{2,1,0:T(8,128)(2,1)S(1)}, bf16[1,128,2048]{2,1,0:T(8,128)(2,1)}, u32[]{:S(2)}) copy-start(bf16[1,128,2048]{2,1,0:T(8,128)(2,1)} %param.12) | copy-start | bytes 1572868
  228.0 42.3 %copy-start.24 = (pred[4,128,16]{2,1,0:T(8,128)(4,1)}, pred[4,128,16]{2,1,0:T(8,128)(4,1)S(1)}, u32[]{:S(2)}) copy-start(pred[4,128,16]{2,1,0:T(8,128)(4,1)S(1)} %copy.62) | copy-start | bytes 24580
  322.8 386.1 %reduce-scatter.3.cloned.1.call-start = ((), (), s32[]{:S(2)}) async-start(), calls=%async_computation.5 | async-start | bytes 28311552 | tf_op jit(solution)/shard_map/reduce_scatter | solution.py:1541
  424.9 51.0 %all-to-all-start.1 = ((bf16[4,128,2048]{2,1,0:T(8,128)(2,1)}), bf16[4,128,2048]{2,1,0:T(8,128)(2,1)S(1)}, u32[]{:S(2)}, u32[]{:S(2)}) async-start(bf16[4,128,2048]{2,1,0:T(8,128)(2,1)} %bitcast.151), calls=%async_computation.1 | async-start | bytes 4194304 | tf_op jit(solution)/shard_map/all_to_all | solution.py:1555
  432.3 2.5 copy-start.8
  461.7 4.8 copy-start.7
  461.7 4.8 copy-start.17
  492.9 4.8 copy-start.30
  492.9 4.9 copy-start.33
  492.9 6.2 copy-start.2
  492.9 9.9 %copy-start.10 = (bf16[128,2048]{1,0:T(8,128)(2,1)S(1)}, bf16[128,2048]{1,0:T(8,128)(2,1)}, u32[]{:S(2)}) copy-start(bf16[128,2048]{1,0:T(8,128)(2,1)} %multiply_convert_fusion.refs_0_) | copy-start | bytes 1572868
  492.9 9.9 %copy-start.27 = (bf16[128,16]{1,0:T(8,128)(2,1)S(1)}, bf16[128,16]{1,0:T(8,128)(2,1)}, u32[]{:S(2)}) copy-start(bf16[128,16]{1,0:T(8,128)(2,1)} %copy-done.26) | copy-start | bytes 12292
  492.9 52.0 %all-to-all-start.2 = ((bf16[1,2,4,64,2048]{4,3,1,0,2:T(8,128)(2,1)}), bf16[1,2,4,64,2048]{4,3,1,0,2:T(8,128)(2,1)}, u32[]{:S(2)}, u32[]{:S(2)}) async-start(bf16[1,2,4,64,2048]{4,3,1,0,2:T(8,128)(2,1)} %bitcast.130), calls=%async_computation.2 | async-start | bytes 4194304 | tf_op jit(solution)/shard_map/all_to_all | solution.py:1578
  499.1 48.6 %collective-permute-start = (bf16[2048,384]{1,0:T(8,128)(2,1)S(1)}, bf16[2048,384]{1,0:T(8,128)(2,1)}, u32[]{:S(2)}, u32[]{:S(2)}) collective-permute-start(bf16[2048,384]{1,0:T(8,128)(2,1)S(1)} %bitcast.124), channel_id=1, source_target_pairs={{0,2},{2,0},{1,3},{3,1},{4,6},{6,4},{5,7},{7,5},{8,10},{10,8},{9,1... | collective-permute-start | bytes 4718600 | tf_op jit(solution)/shard_map/ppermute | solution.py:1570
  600.5 8.8 %copy-start.31 = (f32[1,2048]{1,0:T(1,128)S(1)}, f32[1,2048]{1,0:T(1,128)}, u32[]{:S(2)}) copy-start(f32[1,2048]{1,0:T(1,128)} %reshape.382.gain_ref) | copy-start | bytes 24580
  609.3 9.1 %copy-start.19 = (bf16[2048,384]{1,0:T(8,128)(2,1)S(1)}, bf16[2048,384]{1,0:T(8,128)(2,1)}, u32[]{:S(2)}) copy-start(bf16[2048,384]{1,0:T(8,128)(2,1)} %copy-done.18) | copy-start | bytes 4718596
  613.0 5.4 copy-start.20
  615.8 87.3 %collective-permute-start.1 = (bf16[64,2048]{1,0:T(8,128)(2,1)}, bf16[64,2048]{1,0:T(8,128)(2,1)S(1)}, u32[]{:S(2)}, u32[]{:S(2)}) collective-permute-start(bf16[64,2048]{1,0:T(8,128)(2,1)} %bitcast_add_fusion.1), channel_id=1, source_target_pairs={{0,0},{1,8},{2,16},{3,24},{4,1},{5,9},{6,17},{7,25},{8,2},{9,10},{... | collective-permute-start | bytes 786440 | tf_op jit(solution)/shard_map/ppermute | solution.py:1604
  619.4 73.4 %copy-start.1 = (bf16[4,128,2048]{2,1,0:T(8,128)(2,1)S(1)}, bf16[4,128,2048]{2,1,0:T(8,128)(2,1)}, u32[]{:S(2)}) copy-start(bf16[4,128,2048]{2,1,0:T(8,128)(2,1)} %copy-done) | copy-start | bytes 6291460
  692.8 2.7 copy-start.6
  692.8 3.0 copy-start.14
  (15 other events, 20.4 us)
Sparse Core Ops, SparseCore 0:
  12.5 170.9 all-gather.6
  186.0 129.4 all-gather.4
  322.9 164.9 reduce-scatter.4
  491.4 200.2 reduce-scatter.2

commit v2 on v0

--- a/solution.py
+++ b/solution.py
@@ -385,7 +385,7 @@
 
 def finish_experts(sums, at, total, before=()):
     _, count, rows, units = sums.shape
-    tile = min(128, rows)
+    tile = min(256, rows)
     return pl.pallas_call(
         finish_experts_kernel,
         grid=(count, rows // tile),
@@ -1018,8 +1018,9 @@
     z, u, me = lax.axis_index("blk"), lax.axis_index(ULY), lax.axis_index(ALL)
     far = lax.rem(u + 2, uly)
     near = u + 1 - 2 * lax.rem(u, 2)
-    half = tok_ref.shape[0] // 2
-    parts = (pl.ds(0, half), pl.ds(half, half))
+    rows = tok_ref.shape[0]
+    first = rows * 5 // 8 // 16 * 16
+    parts = (pl.ds(0, first), pl.ds(first, rows - first))
 
     barrier = pltpu.get_barrier_semaphore()
 

time: 709 us -> 713 us (level)
  transfers between devices with their start and end apart: 10 -> 10, of which waited for: 1 -> 1; matrix products, arithmetic and copies ran while one was open for 10% -> 10% of each run, Pallas kernels for 81% -> 80%
where the time goes in v2:
time: 713 us; the launch traced here: 703 us
  Pallas kernels  566 us (79%)
  other arithmetic  36 us (5%)
  starting transfers between devices  24.2 us (3%)
  local copies, waits for them, and re-layouts  22.8 us (3%)
  matrix products  22.8 us (3%)
  between operations  15.6 us (2%)
  waiting for transfers between devices  14.9 us (2%)
    pallas_call x7, Pallas kernels, exchange(): pl.pallas_call(kernel, in_specs=specs + [anywhere] * len(after), out_spec...  275 us
    pallas_call x2, Pallas kernels, experts(): pl.pallas_call(functools.partial(expert_kernel, bool(before), counts), gr...  104 us
    pallas_call x1, Pallas kernels, startup(): pl.pallas_call(startup_kernel, in_specs=[anywhere] * 3, out_specs=[anywhe...  86.9 us
    pallas_call x1, Pallas kernels, turn_gather(): pl.pallas_call(kernel, in_specs=[anywhere] * (2 + len(after)), out_specs=...  36.8 us
    pallas_call x1, Pallas kernels, project_back(): pl.pallas_call(functools.partial(project_back_kernel, head_dim ** (-0.5)...  20.8 us
    reduce_scatter x1, waiting for transfers between devices, per_device(): lax.psum_scatter(grads_others, PLANE, scatter_dimension=0, tiled=False)  14.8 us
  transfers between devices with their start and end apart: 10, of which 1 were waited for; matrix products, arithmetic and copies ran while one was open for 10% of the time, Pallas kernels for 80%

profile of v2, /device:TPU:0, one launch (start us, length us, event | category | flops | bytes accessed | tf_op | source)
XLA Modules:
  0.0 702.6 jit_solution(8870772309337182092)
XLA Ops:
  7.2 2.8 fusion.26
  12.4 3.0 collective-permute-start.1
  15.4 3.6 collective-permute-start
  21.8 86.9 %startup.1 = (bf16[2,16,64,384]{3,2,1,0:T(8,128)(2,1)}, bf16[2,16,32,128]{3,2,1,0:T(8,128)(2,1)}, bf16[4,4,128,2048]{3,2,1,0:T(8,128)(2,1)}) custom-call(bf16[16,64,384]{2,1,0:T(8,128)(2,1)} %reshape.355.head_ref, bf16[32,128]{1,0:T(8,128)(2,1)} %fusion.23.extra_ref, bf16[128,2048]{1,0:T(8,128)(2,1)} %bitcast.130), custom_call_target="tpu_custom_call" | custom-call | tf_op jit(solution)/shard_map/startup/pallas_call | solution.py:1175
  108.7 3.1 pad_maximum_fusion
  114.6 8.5 %all-to-all-start = ((bf16[4,2,64,2048]{3,2,1,0:T(8,128)(2,1)}), bf16[4,2,64,2048]{3,2,1,0:T(8,128)(2,1)S(1)}, u32[]{:S(2)}, u32[]{:S(2)}) async-start(bf16[4,2,64,2048]{3,2,1,0:T(8,128)(2,1)} %broadcast_in_dim.41), calls=%async_computation | async-start | bytes 4194304 | tf_op jit(solution)/shard_map/all_to_all | solution.py:1470
  128.9 13.4 %project.1 = (bf16[2048,2048]{1,0:T(8,128)(2,1)}, bf16[2048,384]{1,0:T(8,128)(2,1)}, f32[2048,256]{1,0:T(8,128)}) custom-call(bf16[2048,2048]{1,0:T(8,128)(2,1)} %bitcast.132, f32[1,2048]{1,0:T(1,128)} %reshape.381.gain_ref, bf16[2048,384]{1,0:T(8,128)(2,1)} %bitcast.122, f32[2048,128]{1,0:T(8,128)} %bitcast.136, ...), custom_call_target="tpu_custom_call" | custom-call | tf_op jit(solution)/shard_map/project/pallas_call | solution.py:442
  142.3 9.8 %attend.1 = (bf16[1,2048,128]{2,1,0:T(8,128)(2,1)}, f32[1,2048,128]{2,1,0:T(8,128)}, f32[1,1,2048]{2,1,0:T(1,128)}, f32[1,1,2048]{2,1,0:T(1,128)}) custom-call(bf16[1,2048,384]{2,1,0:T(8,128)(2,1)} %bitcast.186, bf16[1,2048,384]{2,1,0:T(8,128)(2,1)} %bitcast.187, bf16[1,2048,384]{2,1,0:T(8,128)(2,1)} %bitcast.188, s32[1,2048]{1,0:T(1,128)} %sq_ref.3, ...), custom_call_target="tpu_custom_call" | custom-call | flops 2147483648 | bytes 4194304 | tf_op jit(solution)/shard_map/attend/pallas_call | solution.py:179
  152.2 29.3 %exchange.7 = bf16[4,512,128]{2,1,0:T(8,128)(2,1)} custom-call(bf16[4,512,128]{2,1,0:T(8,128)(2,1)} %bitcast.162), custom_call_target="tpu_custom_call" | custom-call | tf_op jit(solution)/shard_map/exchange/pallas_call | solution.py:872
  182.5 2.6 bitcast_convert_fusion
  185.1 42.4 %exchange.8 = (f32[128,2048]{1,0:T(8,128)}, bf16[4,128,2048]{2,1,0:T(8,128)(2,1)}, s32[4,8,128]{2,1,0:T(8,128)}) custom-call(bf16[4,128,2048]{2,1,0:T(8,128)(2,1)} %bitcast.146, bf16[128,2048]{1,0:T(8,128)(2,1)} %bitcast.134, s32[8,128]{1,0:T(8,128)} %bitcast.176), custom_call_target="tpu_custom_call" | custom-call | tf_op jit(solution)/shard_map/exchange/pallas_call | solution.py:872
  231.0 36.8 %turn_gather.1 = (bf16[4,128,2048]{2,1,0:T(8,128)(2,1)}, bf16[2048,512]{1,0:T(8,128)(2,1)}, bf16[2048,512]{1,0:T(8,128)(2,1)}) custom-call(bf16[128,2048]{1,0:T(8,128)(2,1)} %multiply_convert_fusion.refs_0_, bf16[4,128,2048]{2,1,0:T(8,128)(2,1)} %get-tuple-element.81.refs_1_), custom_call_target="tpu_custom_call" | custom-call | tf_op jit(solution)/shard_map/turn_gather/pallas_call | solution.py:988
  267.7 2.3 fusion.28
  271.7 51.5 %experts.2 = (bf16[512,2048]{1,0:T(8,128)(2,1)}, bf16[512,2048]{1,0:T(8,128)(2,1)}, f32[2,512,1]{2,1,0:T(8,128)}, bf16[8,3,2,256,1024]{4,3,2,1,0:T(8,128)(2,1)}) custom-call(bf16[512,2048]{1,0:T(8,128)(2,1)} %bitcast.148, bf16[2048,512]{1,0:T(8,128)(2,1)} %get-tuple-element.83.refs_1_, bf16[512,2048]{1,0:T(8,128)(2,1)} %bitcast.144, ...), custom_call_target="tpu_custom_call" | custom-call | flops 38654705664 | bytes 50331648 | tf_op jit(solution)/shard_map/experts/pallas_call | solution.py:340
  323.5 52.8 %experts.3 = (bf16[512,2048]{1,0:T(8,128)(2,1)}, bf16[512,2048]{1,0:T(8,128)(2,1)}, f32[2,512,1]{2,1,0:T(8,128)}, bf16[8,3,2,256,1024]{4,3,2,1,0:T(8,128)(2,1)}) custom-call(bf16[512,2048]{1,0:T(8,128)(2,1)} %bitcast.149, bf16[2048,512]{1,0:T(8,128)(2,1)} %get-tuple-element.83.refs_1_, bf16[512,2048]{1,0:T(8,128)(2,1)} %bitcast.145, ...), custom_call_target="tpu_custom_call" | custom-call | flops 38654705664 | bytes 50331648 | tf_op jit(solution)/shard_map/experts/pallas_call | solution.py:340
  379.4 46.5 %exchange.9 = (bf16[4,128,2048]{2,1,0:T(8,128)(2,1)}, f32[4,4,128]{2,1,0:T(4,128)}) custom-call(bf16[4,128,2048]{2,1,0:T(8,128)(2,1)} %bitcast.153, f32[4,4,128]{2,1,0:T(4,128)} %maximum_bitcast_fusion.refs_1_), custom_call_target="tpu_custom_call" | custom-call | tf_op jit(solution)/shard_map/exchange/pallas_call | solution.py:872
  425.8 3.9 all-to-all-start.1
  438.2 29.3 %exchange.10 = bf16[4,128,2048]{2,1,0:T(8,128)(2,1)} custom-call(bf16[128,2048]{1,0:T(8,128)(2,1)} %fusion.24.refs_0_), custom_call_target="tpu_custom_call" | custom-call | tf_op jit(solution)/shard_map/exchange/pallas_call | solution.py:872
  467.4 3.5 collective-permute-start.2
  472.2 3.2 convolution_convert_fusion
  478.2 2.2 fusion.2.refs_0_
  481.6 27.3 %exchange.11 = (bf16[4,512,128]{2,1,0:T(8,128)(2,1)}, bf16[4,64,2048]{2,1,0:T(8,128)(2,1)}) custom-call(bf16[4,512,128]{2,1,0:T(8,128)(2,1)} %fusion.2.refs_0_, bf16[4,64,2048]{2,1,0:T(8,128)(2,1)} %dynamic-slice_bitcast_fusion.refs_1_, bf16[4,128,2048]{2,1,0:T(8,128)(2,1)} %copy-done), custom_call_target="tpu_custom_call" | custom-call | tf_op jit(solution)/shard_map/exchange/pallas_call | solution.py:872
  508.9 20.8 %project_back.1 = (bf16[2048,384]{1,0:T(8,128)(2,1)}, f32[2,128]{1,0:T(2,128)}) custom-call(bf16[2048,384]{1,0:T(8,128)(2,1)} %get-tuple-element.76.q_ref.k_ref.v_ref, bf16[2048,384]{1,0:T(8,128)(2,1)} %get-tuple-element.76.q_ref.k_ref.v_ref, bf16[2048,384]{1,0:T(8,128)(2,1)} %get-tuple-element.76.q_ref.k_ref.v_ref, bf16[2048,128]{1,0:T(8,128)(2,1)} %bitcast.189, ...), custom_call_target="tpu_custom_call" | custom-call | flops 5368709120 | bytes 10485760 | tf_op jit(solution)/shard_map/project_back/pallas_call | solution.py:526
  529.8 10.9 %convolution_convert_fusion.1 = bf16[2048,384]{1,0:T(8,128)(2,1)S(1)} fusion(bf16[2048,2048]{1,0:T(8,128)(2,1)} %get-tuple-element.104, bf16[2048,384]{1,0:T(8,128)(2,1)} %get-tuple-element.103), kind=kOutput, calls=%fused_computation.7 | convolution fusion | flops 3222011904 | bytes 11534336 | tf_op jit(solution)/shard_map/dot_general | solution.py:82
  543.5 27.7 %exchange.12 = (bf16[4,4,128,384]{3,2,1,0:T(8,128)(2,1)}, bf16[1024,384]{1,0:T(8,128)(2,1)}, bf16[2048,384]{1,0:T(8,128)(2,1)}, bf16[2048,384]{1,0:T(8,128)(2,1)}, bf16[4,64,2048]{2,1,0:T(8,128)(2,1)}) custom-call(bf16[4,4,128,384]{3,2,1,0:T(8,128)(2,1)} %bitcast.156, bf16[1024,384]{1,0:T(8,128)(2,1)} %dynamic-slice_bitcast_fusion.1.refs_1_, ...), custom_call_target="tpu_custom_call" | custom-call | tf_op jit(solution)/shard_map/exchange/pallas_call | solution.py:872
  571.2 8.6 %hidden_back.1 = (bf16[4,128,2048]{2,1,0:T(8,128)(2,1)}, f32[1,2048]{1,0:T(1,128)}) custom-call(bf16[4,512,384]{2,1,0:T(8,128)(2,1)} %bitcast.157, bf16[2048,384]{1,0:T(8,128)(2,1)} %bitcast.125, bf16[2048,384]{1,0:T(8,128)(2,1)} %get-tuple-element.108.near_ref, bf16[2048,384]{1,0:T(8,128)(2,1)} %collective-permute-done.2.refs_3_.far_ref, ...), custom_call_target="tpu_custom_call" | custom-call | tf_op jit(solution)/shard_map/hidden_back/pallas_call | solution.py:590
  586.9 72.2 %exchange.13 = (bf16[4,128,2048]{2,1,0:T(8,128)(2,1)}, f32[32,16,128]{2,1,0:T(8,128)}, bf16[16,64,384]{2,1,0:T(8,128)(2,1)}) custom-call(bf16[4,128,2048]{2,1,0:T(8,128)(2,1)} %get-tuple-element.110.refs_0_, f32[32,16,128]{2,1,0:T(8,128)} %select_maximum_fusion.refs_1_, bf16[16,64,384]{2,1,0:T(8,128)(2,1)} %bitcast.141), custom_call_target="tpu_custom_call" | custom-call | tf_op jit(solution)/shard_map/exchange/pallas_call | solution.py:872
  660.2 2.7 convert_reduce_fusion
  667.5 2.5 merge_heads.1
  672.3 4.2 finish_experts.2
  676.6 14.8 %reduce-scatter.3.cloned.1.call-done = bf16[1,3,2,256,1024]{4,3,2,1,0:T(8,128)(2,1)} async-done(((bf16[8,3,2,256,1024]{4,3,2,1,0:T(8,128)(2,1)}), bf16[1,3,2,256,1024]{4,3,2,1,0:T(8,128)(2,1)}) %reduce-scatter.3.cloned.1.call-update) | async-done | bytes 3145744 | tf_op jit(solution)/shard_map/reduce_scatter | solution.py:1524
  691.3 4.2 finish_experts.3
  (176 shorter events, 53.7 us)
Async XLA Ops:
  7.2 264.5 %all-gather.7.cloned.1.call-start = ((), (), s32[]{:S(2)}) async-start(), calls=%async_computation.7 | async-start | bytes 28311552 | tf_op jit(solution)/shard_map/all_gather | solution.py:1452
  7.2 2.9 copy-start.11
  12.4 6.7 copy-start.12
  12.4 311.1 %all-gather.5.cloned.1.call-start = ((), (), s32[]{:S(2)}) async-start(), calls=%async_computation.6 | async-start | bytes 28311552 | tf_op jit(solution)/shard_map/all_gather | solution.py:1452
  12.4 96.2 %collective-permute-start.1 = (bf16[64,2048]{1,0:T(8,128)(2,1)}, bf16[64,2048]{1,0:T(8,128)(2,1)S(1)}, u32[]{:S(2)}, u32[]{:S(2)}) collective-permute-start(bf16[64,2048]{1,0:T(8,128)(2,1)} %param.16), channel_id=1, source_target_pairs={{0,16},{8,17},{16,18},{24,19},{1,20},{9,21},{17,22},{25,23},{2,24}... | collective-permute-start | bytes 786440 | tf_op jit(solution)/shard_map/ppermute | solution.py:1446
  15.4 93.2 %collective-permute-start = (bf16[64,2048]{1,0:T(8,128)(2,1)}, bf16[64,2048]{1,0:T(8,128)(2,1)}, u32[]{:S(2)}, u32[]{:S(2)}) collective-permute-start(bf16[64,2048]{1,0:T(8,128)(2,1)} %param.16), channel_id=1, source_target_pairs={{0,0},{8,1},{16,2},{24,3},{1,4},{9,5},{17,6},{25,7},{2,8},{10,9},{... | collective-permute-start | bytes 786440 | tf_op jit(solution)/shard_map/ppermute | solution.py:1445
  114.6 8.6 %copy-start.37 = (bf16[2,128]{1,0:T(2,128)(2,1)S(1)}, bf16[2,128]{1,0:T(2,128)(2,1)}, u32[]{:S(2)}) copy-start(bf16[2,128]{1,0:T(2,128)(2,1)} %param.19) | copy-start | bytes 1540
  114.6 9.6 %copy-start.26 = (s32[1,2048]{1,0:T(1,128)S(1)}, s32[1,2048]{1,0:T(1,128)}, u32[]{:S(2)}) copy-start(s32[1,2048]{1,0:T(1,128)} %sq_ref.3) | copy-start | bytes 24580
  114.6 66.8 %all-to-all-start = ((bf16[4,2,64,2048]{3,2,1,0:T(8,128)(2,1)}), bf16[4,2,64,2048]{3,2,1,0:T(8,128)(2,1)S(1)}, u32[]{:S(2)}, u32[]{:S(2)}) async-start(bf16[4,2,64,2048]{3,2,1,0:T(8,128)(2,1)} %broadcast_in_dim.41), calls=%async_computation | async-start | bytes 4194304 | tf_op jit(solution)/shard_map/all_to_all | solution.py:1470
  123.2 549.2 %reduce-scatter.5.cloned.1.call-start = ((), (), s32[]{:S(2)}) async-start(), calls=%async_computation.5 | async-start | bytes 28311552 | tf_op jit(solution)/shard_map/reduce_scatter | solution.py:1520
  125.6 2.3 copy-start.24
  181.6 3.5 copy-start.15
  185.1 43.3 %copy-start.7 = (bf16[1,128,2048]{2,1,0:T(8,128)(2,1)S(1)}, bf16[1,128,2048]{2,1,0:T(8,128)(2,1)}, u32[]{:S(2)}) copy-start(bf16[1,128,2048]{2,1,0:T(8,128)(2,1)} %param.12) | copy-start | bytes 1572868
  228.4 42.2 %copy-start.20 = (pred[4,128,16]{2,1,0:T(8,128)(4,1)}, pred[4,128,16]{2,1,0:T(8,128)(4,1)S(1)}, u32[]{:S(2)}) copy-start(pred[4,128,16]{2,1,0:T(8,128)(4,1)S(1)} %copy.61) | copy-start | bytes 24580
  230.0 37.7 %copy-start.27 = (f32[128]{0:T(128)}, f32[128]{0:T(128)S(1)}, u32[]{:S(2)}) copy-start(f32[128]{0:T(128)S(1)} %add_rsqrt_fusion.1) | copy-start | bytes 1540
  323.2 368.1 %reduce-scatter.3.cloned.1.call-start = ((), (), s32[]{:S(2)}) async-start(), calls=%async_computation.4 | async-start | bytes 28311552 | tf_op jit(solution)/shard_map/reduce_scatter | solution.py:1524
  425.8 54.5 %all-to-all-start.1 = ((bf16[4,128,2048]{2,1,0:T(8,128)(2,1)}), bf16[4,128,2048]{2,1,0:T(8,128)(2,1)S(1)}, u32[]{:S(2)}, u32[]{:S(2)}) async-start(bf16[4,128,2048]{2,1,0:T(8,128)(2,1)} %bitcast.152), calls=%async_computation.1 | async-start | bytes 4194304 | tf_op jit(solution)/shard_map/all_to_all | solution.py:1538
  431.6 3.8 copy-start.28
  434.5 2.5 copy-start.9
  438.2 32.8 %copy-start.23 = (bf16[128,16]{1,0:T(8,128)(2,1)S(1)}, bf16[128,16]{1,0:T(8,128)(2,1)}, u32[]{:S(2)}) copy-start(bf16[128,16]{1,0:T(8,128)(2,1)} %copy-done.22) | copy-start | bytes 12292
  467.4 76.0 %collective-permute-start.2 = (bf16[2048,384]{1,0:T(8,128)(2,1)}, bf16[2048,384]{1,0:T(8,128)(2,1)}, u32[]{:S(2)}, u32[]{:S(2)}) collective-permute-start(bf16[2048,384]{1,0:T(8,128)(2,1)} %bitcast.123), channel_id=1, source_target_pairs={{0,2},{2,0},{1,3},{3,1},{4,6},{6,4},{5,7},{7,5},{8,10},{10,8},{9,1... | collective-permute-start | bytes 4718600 | tf_op jit(solution)/shard_map/ppermute | solution.py:1553
  472.2 4.8 copy-start.16
  475.4 2.7 copy-start.6
  529.8 11.9 %copy-start.5 = (bf16[4,128,2048]{2,1,0:T(8,128)(2,1)S(1)}, bf16[4,128,2048]{2,1,0:T(8,128)(2,1)}, u32[]{:S(2)}) copy-start(bf16[4,128,2048]{2,1,0:T(8,128)(2,1)} %copy-done.4) | copy-start | bytes 6291460
  571.2 8.7 %copy-start.25 = (f32[1,2048]{1,0:T(1,128)S(1)}, f32[1,2048]{1,0:T(1,128)}, u32[]{:S(2)}) copy-start(f32[1,2048]{1,0:T(1,128)} %reshape.381.gain_ref) | copy-start | bytes 24580
  579.9 4.2 copy-start.33
  579.9 4.2 copy-start.34
  582.7 87.8 %collective-permute-start.3 = (bf16[64,2048]{1,0:T(8,128)(2,1)S(1)}, bf16[64,2048]{1,0:T(8,128)(2,1)}, u32[]{:S(2)}, u32[]{:S(2)}) collective-permute-start(bf16[64,2048]{1,0:T(8,128)(2,1)S(1)} %reduce_sum.121), channel_id=1, source_target_pairs={{0,0},{1,8},{2,16},{3,24},{4,1},{5,9},{6,17},{7,25},{8,2},{9,10},{... | collective-permute-start | bytes 786440 | tf_op jit(solution)/shard_map/ppermute | solution.py:1591
  586.9 73.2 %copy-start.1 = (bf16[4,128,2048]{2,1,0:T(8,128)(2,1)S(1)}, bf16[4,128,2048]{2,1,0:T(8,128)(2,1)}, u32[]{:S(2)}) copy-start(bf16[4,128,2048]{2,1,0:T(8,128)(2,1)} %copy-done) | copy-start | bytes 6291460
  660.2 2.7 copy-start.8
  660.2 2.7 copy-start.32
  660.2 3.0 copy-start.13
  (16 other events, 24.7 us)
Sparse Core Ops, SparseCore 0:
  12.5 172.2 all-gather.6
  187.3 129.4 all-gather.4
  323.4 185.7 reduce-scatter.4
  512.7 178.6 reduce-scatter.2

commit v3 on v0

--- a/solution.py
+++ b/solution.py
@@ -385,7 +385,7 @@
 
 def finish_experts(sums, at, total, before=()):
     _, count, rows, units = sums.shape
-    tile = min(128, rows)
+    tile = min(256, rows)
     return pl.pallas_call(
         finish_experts_kernel,
         grid=(count, rows // tile),
@@ -1103,7 +1103,6 @@
         extra(step).start()
         head(step).start()
 
-    each(here, start_head)
     ways = (1, 0)
     b_y().start()
     for stream in range(2):
@@ -1113,6 +1112,7 @@
     to_near(0, 0, 0).start()
     to_near(0, 0, 1).start()
 
+    each(here, start_head)
     for copy in own:
         copy.start()
     b_y().wait_recv()

time: 709 us -> 708 us (level)
  no operation moved by 1% of the time
where the time goes in v3:
time: 708 us; the launch traced here: 697 us
  Pallas kernels  568 us (80%)
  other arithmetic  36.3 us (5%)
  local copies, waits for them, and re-layouts  22.9 us (3%)
  matrix products  22.7 us (3%)
  starting transfers between devices  20.4 us (3%)
  between operations  15.6 us (2%)
  waiting for transfers between devices  11.3 us (2%)
    pallas_call x7, Pallas kernels, exchange(): pl.pallas_call(kernel, in_specs=specs + [anywhere] * len(after), out_spec...  278 us
    pallas_call x2, Pallas kernels, experts(): pl.pallas_call(functools.partial(expert_kernel, bool(before), counts), gr...  104 us
    pallas_call x1, Pallas kernels, startup(): pl.pallas_call(startup_kernel, in_specs=[anywhere] * 3, out_specs=[anywhe...  84.7 us
    pallas_call x1, Pallas kernels, turn_gather(): pl.pallas_call(kernel, in_specs=[anywhere] * (2 + len(after)), out_specs=...  36.6 us
    pallas_call x1, Pallas kernels, project_back(): pl.pallas_call(functools.partial(project_back_kernel, head_dim ** (-0.5)...  20.8 us
  transfers between devices with their start and end apart: 10, of which 1 were waited for; matrix products, arithmetic and copies ran while one was open for 10% of the time, Pallas kernels for 81%

profile of v3, /device:TPU:0, one launch (start us, length us, event | category | flops | bytes accessed | tf_op | source)
XLA Modules:
  0.0 697.2 jit_solution(18014400760366714545)
XLA Ops:
  7.2 2.8 fusion.26
  12.4 3.0 collective-permute-start.1
  15.4 3.6 collective-permute-start
  21.8 84.7 %startup.1 = (bf16[2,16,64,384]{3,2,1,0:T(8,128)(2,1)}, bf16[2,16,32,128]{3,2,1,0:T(8,128)(2,1)}, bf16[4,4,128,2048]{3,2,1,0:T(8,128)(2,1)}) custom-call(bf16[16,64,384]{2,1,0:T(8,128)(2,1)} %reshape.355.head_ref, bf16[32,128]{1,0:T(8,128)(2,1)} %fusion.23.extra_ref, bf16[128,2048]{1,0:T(8,128)(2,1)} %bitcast.130), custom_call_target="tpu_custom_call" | custom-call | tf_op jit(solution)/shard_map/startup/pallas_call | solution.py:1174
  106.5 3.3 pad_maximum_fusion
  112.7 6.0 all-to-all-start
  124.4 13.1 %project.1 = (bf16[2048,2048]{1,0:T(8,128)(2,1)}, bf16[2048,384]{1,0:T(8,128)(2,1)}, f32[2048,256]{1,0:T(8,128)}) custom-call(bf16[2048,2048]{1,0:T(8,128)(2,1)} %bitcast.132, f32[1,2048]{1,0:T(1,128)} %reshape.381.gain_ref, bf16[2048,384]{1,0:T(8,128)(2,1)} %bitcast.122, f32[2048,128]{1,0:T(8,128)} %bitcast.136, ...), custom_call_target="tpu_custom_call" | custom-call | tf_op jit(solution)/shard_map/project/pallas_call | solution.py:442
  137.4 9.9 %attend.1 = (bf16[1,2048,128]{2,1,0:T(8,128)(2,1)}, f32[1,2048,128]{2,1,0:T(8,128)}, f32[1,1,2048]{2,1,0:T(1,128)}, f32[1,1,2048]{2,1,0:T(1,128)}) custom-call(bf16[1,2048,384]{2,1,0:T(8,128)(2,1)} %bitcast.186, bf16[1,2048,384]{2,1,0:T(8,128)(2,1)} %bitcast.187, bf16[1,2048,384]{2,1,0:T(8,128)(2,1)} %bitcast.188, s32[1,2048]{1,0:T(1,128)} %sq_ref.3, ...), custom_call_target="tpu_custom_call" | custom-call | flops 2147483648 | bytes 4194304 | tf_op jit(solution)/shard_map/attend/pallas_call | solution.py:179
  147.3 29.6 %exchange.7 = bf16[4,512,128]{2,1,0:T(8,128)(2,1)} custom-call(bf16[4,512,128]{2,1,0:T(8,128)(2,1)} %bitcast.162), custom_call_target="tpu_custom_call" | custom-call | tf_op jit(solution)/shard_map/exchange/pallas_call | solution.py:872
  178.0 2.6 bitcast_convert_fusion
  180.6 42.2 %exchange.8 = (f32[128,2048]{1,0:T(8,128)}, bf16[4,128,2048]{2,1,0:T(8,128)(2,1)}, s32[4,8,128]{2,1,0:T(8,128)}) custom-call(bf16[4,128,2048]{2,1,0:T(8,128)(2,1)} %bitcast.146, bf16[128,2048]{1,0:T(8,128)(2,1)} %bitcast.134, s32[8,128]{1,0:T(8,128)} %bitcast.176), custom_call_target="tpu_custom_call" | custom-call | tf_op jit(solution)/shard_map/exchange/pallas_call | solution.py:872
  226.3 36.6 %turn_gather.1 = (bf16[4,128,2048]{2,1,0:T(8,128)(2,1)}, bf16[2048,512]{1,0:T(8,128)(2,1)}, bf16[2048,512]{1,0:T(8,128)(2,1)}) custom-call(bf16[128,2048]{1,0:T(8,128)(2,1)} %multiply_convert_fusion.refs_0_, bf16[4,128,2048]{2,1,0:T(8,128)(2,1)} %get-tuple-element.81.refs_1_), custom_call_target="tpu_custom_call" | custom-call | tf_op jit(solution)/shard_map/turn_gather/pallas_call | solution.py:988
  262.9 2.3 fusion.28
  266.8 51.4 %experts.2 = (bf16[512,2048]{1,0:T(8,128)(2,1)}, bf16[512,2048]{1,0:T(8,128)(2,1)}, f32[2,512,1]{2,1,0:T(8,128)}, bf16[8,3,2,256,1024]{4,3,2,1,0:T(8,128)(2,1)}) custom-call(bf16[512,2048]{1,0:T(8,128)(2,1)} %bitcast.148, bf16[2048,512]{1,0:T(8,128)(2,1)} %get-tuple-element.83.refs_1_, bf16[512,2048]{1,0:T(8,128)(2,1)} %bitcast.144, ...), custom_call_target="tpu_custom_call" | custom-call | flops 38654705664 | bytes 50331648 | tf_op jit(solution)/shard_map/experts/pallas_call | solution.py:340
  318.6 52.8 %experts.3 = (bf16[512,2048]{1,0:T(8,128)(2,1)}, bf16[512,2048]{1,0:T(8,128)(2,1)}, f32[2,512,1]{2,1,0:T(8,128)}, bf16[8,3,2,256,1024]{4,3,2,1,0:T(8,128)(2,1)}) custom-call(bf16[512,2048]{1,0:T(8,128)(2,1)} %bitcast.149, bf16[2048,512]{1,0:T(8,128)(2,1)} %get-tuple-element.83.refs_1_, bf16[512,2048]{1,0:T(8,128)(2,1)} %bitcast.145, ...), custom_call_target="tpu_custom_call" | custom-call | flops 38654705664 | bytes 50331648 | tf_op jit(solution)/shard_map/experts/pallas_call | solution.py:340
  374.4 47.0 %exchange.9 = (bf16[4,128,2048]{2,1,0:T(8,128)(2,1)}, f32[4,4,128]{2,1,0:T(4,128)}) custom-call(bf16[4,128,2048]{2,1,0:T(8,128)(2,1)} %bitcast.153, f32[4,4,128]{2,1,0:T(4,128)} %maximum_bitcast_fusion.refs_1_), custom_call_target="tpu_custom_call" | custom-call | tf_op jit(solution)/shard_map/exchange/pallas_call | solution.py:872
  421.4 3.9 all-to-all-start.1
  433.7 30.5 %exchange.10 = bf16[4,128,2048]{2,1,0:T(8,128)(2,1)} custom-call(bf16[128,2048]{1,0:T(8,128)(2,1)} %fusion.24.refs_0_), custom_call_target="tpu_custom_call" | custom-call | tf_op jit(solution)/shard_map/exchange/pallas_call | solution.py:872
  464.2 2.3 collective-permute-start.2
  467.8 3.2 convolution_convert_fusion
  473.7 2.2 fusion.2.refs_0_
  477.2 27.8 %exchange.11 = (bf16[4,512,128]{2,1,0:T(8,128)(2,1)}, bf16[4,64,2048]{2,1,0:T(8,128)(2,1)}) custom-call(bf16[4,512,128]{2,1,0:T(8,128)(2,1)} %fusion.2.refs_0_, bf16[4,64,2048]{2,1,0:T(8,128)(2,1)} %dynamic-slice_bitcast_fusion.refs_1_, bf16[4,128,2048]{2,1,0:T(8,128)(2,1)} %copy-done), custom_call_target="tpu_custom_call" | custom-call | tf_op jit(solution)/shard_map/exchange/pallas_call | solution.py:872
  505.0 20.8 %project_back.1 = (bf16[2048,384]{1,0:T(8,128)(2,1)}, f32[2,128]{1,0:T(2,128)}) custom-call(bf16[2048,384]{1,0:T(8,128)(2,1)} %get-tuple-element.76.q_ref.k_ref.v_ref, bf16[2048,384]{1,0:T(8,128)(2,1)} %get-tuple-element.76.q_ref.k_ref.v_ref, bf16[2048,384]{1,0:T(8,128)(2,1)} %get-tuple-element.76.q_ref.k_ref.v_ref, bf16[2048,128]{1,0:T(8,128)(2,1)} %bitcast.189, ...), custom_call_target="tpu_custom_call" | custom-call | flops 5368709120 | bytes 10485760 | tf_op jit(solution)/shard_map/project_back/pallas_call | solution.py:526
  525.8 10.8 %convolution_convert_fusion.1 = bf16[2048,384]{1,0:T(8,128)(2,1)S(1)} fusion(bf16[2048,2048]{1,0:T(8,128)(2,1)} %get-tuple-element.104, bf16[2048,384]{1,0:T(8,128)(2,1)} %get-tuple-element.103), kind=kOutput, calls=%fused_computation.7 | convolution fusion | flops 3222011904 | bytes 11534336 | tf_op jit(solution)/shard_map/dot_general | solution.py:82
  539.5 28.8 %exchange.12 = (bf16[4,4,128,384]{3,2,1,0:T(8,128)(2,1)}, bf16[1024,384]{1,0:T(8,128)(2,1)}, bf16[2048,384]{1,0:T(8,128)(2,1)}, bf16[2048,384]{1,0:T(8,128)(2,1)}, bf16[4,64,2048]{2,1,0:T(8,128)(2,1)}) custom-call(bf16[4,4,128,384]{3,2,1,0:T(8,128)(2,1)} %bitcast.156, bf16[1024,384]{1,0:T(8,128)(2,1)} %dynamic-slice_bitcast_fusion.1.refs_1_, ...), custom_call_target="tpu_custom_call" | custom-call | tf_op jit(solution)/shard_map/exchange/pallas_call | solution.py:872
  568.3 9.2 %hidden_back.1 = (bf16[4,128,2048]{2,1,0:T(8,128)(2,1)}, f32[1,2048]{1,0:T(1,128)}) custom-call(bf16[4,512,384]{2,1,0:T(8,128)(2,1)} %bitcast.157, bf16[2048,384]{1,0:T(8,128)(2,1)} %bitcast.125, bf16[2048,384]{1,0:T(8,128)(2,1)} %get-tuple-element.108.near_ref, bf16[2048,384]{1,0:T(8,128)(2,1)} %collective-permute-done.2.refs_3_.far_ref, ...), custom_call_target="tpu_custom_call" | custom-call | tf_op jit(solution)/shard_map/hidden_back/pallas_call | solution.py:590
  584.7 72.6 %exchange.13 = (bf16[4,128,2048]{2,1,0:T(8,128)(2,1)}, f32[32,16,128]{2,1,0:T(8,128)}, bf16[16,64,384]{2,1,0:T(8,128)(2,1)}) custom-call(bf16[4,128,2048]{2,1,0:T(8,128)(2,1)} %get-tuple-element.110.refs_0_, f32[32,16,128]{2,1,0:T(8,128)} %select_maximum_fusion.refs_1_, bf16[16,64,384]{2,1,0:T(8,128)(2,1)} %bitcast.141), custom_call_target="tpu_custom_call" | custom-call | tf_op jit(solution)/shard_map/exchange/pallas_call | solution.py:872
  658.4 2.6 convert_reduce_fusion
  665.7 2.5 merge_heads.1
  670.5 4.2 finish_experts.2
  674.8 11.2 %reduce-scatter.3.cloned.1.call-done = bf16[1,3,2,256,1024]{4,3,2,1,0:T(8,128)(2,1)} async-done(((bf16[8,3,2,256,1024]{4,3,2,1,0:T(8,128)(2,1)}), bf16[1,3,2,256,1024]{4,3,2,1,0:T(8,128)(2,1)}) %reduce-scatter.3.cloned.1.call-update) | async-done | bytes 3145744 | tf_op jit(solution)/shard_map/reduce_scatter | solution.py:1523
  686.0 4.2 finish_experts.3
  (176 shorter events, 53.9 us)
Async XLA Ops:
  7.2 259.7 %all-gather.7.cloned.1.call-start = ((), (), s32[]{:S(2)}) async-start(), calls=%async_computation.7 | async-start | bytes 28311552 | tf_op jit(solution)/shard_map/all_gather | solution.py:1451
  7.2 2.9 copy-start.11
  12.4 6.7 copy-start.12
  12.4 306.2 %all-gather.5.cloned.1.call-start = ((), (), s32[]{:S(2)}) async-start(), calls=%async_computation.6 | async-start | bytes 28311552 | tf_op jit(solution)/shard_map/all_gather | solution.py:1451
  12.4 94.0 %collective-permute-start.1 = (bf16[64,2048]{1,0:T(8,128)(2,1)}, bf16[64,2048]{1,0:T(8,128)(2,1)S(1)}, u32[]{:S(2)}, u32[]{:S(2)}) collective-permute-start(bf16[64,2048]{1,0:T(8,128)(2,1)} %param.16), channel_id=1, source_target_pairs={{0,16},{8,17},{16,18},{24,19},{1,20},{9,21},{17,22},{25,23},{2,24}... | collective-permute-start | bytes 786440 | tf_op jit(solution)/shard_map/ppermute | solution.py:1445
  15.4 91.0 %collective-permute-start = (bf16[64,2048]{1,0:T(8,128)(2,1)}, bf16[64,2048]{1,0:T(8,128)(2,1)}, u32[]{:S(2)}, u32[]{:S(2)}) collective-permute-start(bf16[64,2048]{1,0:T(8,128)(2,1)} %param.16), channel_id=1, source_target_pairs={{0,0},{8,1},{16,2},{24,3},{1,4},{9,5},{17,6},{25,7},{2,8},{10,9},{... | collective-permute-start | bytes 786440 | tf_op jit(solution)/shard_map/ppermute | solution.py:1444
  112.7 6.0 copy-start.37
  112.7 7.0 %copy-start.26 = (s32[1,2048]{1,0:T(1,128)S(1)}, s32[1,2048]{1,0:T(1,128)}, u32[]{:S(2)}) copy-start(s32[1,2048]{1,0:T(1,128)} %sq_ref.3) | copy-start | bytes 24580
  112.7 64.3 %all-to-all-start = ((bf16[4,2,64,2048]{3,2,1,0:T(8,128)(2,1)}), bf16[4,2,64,2048]{3,2,1,0:T(8,128)(2,1)S(1)}, u32[]{:S(2)}, u32[]{:S(2)}) async-start(bf16[4,2,64,2048]{3,2,1,0:T(8,128)(2,1)} %broadcast_in_dim.41), calls=%async_computation | async-start | bytes 4194304 | tf_op jit(solution)/shard_map/all_to_all | solution.py:1469
  118.6 551.9 %reduce-scatter.5.cloned.1.call-start = ((), (), s32[]{:S(2)}) async-start(), calls=%async_computation.5 | async-start | bytes 28311552 | tf_op jit(solution)/shard_map/reduce_scatter | solution.py:1519
  121.1 2.3 copy-start.24
  177.1 3.5 copy-start.15
  180.6 43.2 %copy-start.7 = (bf16[1,128,2048]{2,1,0:T(8,128)(2,1)S(1)}, bf16[1,128,2048]{2,1,0:T(8,128)(2,1)}, u32[]{:S(2)}) copy-start(bf16[1,128,2048]{2,1,0:T(8,128)(2,1)} %param.12) | copy-start | bytes 1572868
  223.7 42.0 %copy-start.20 = (pred[4,128,16]{2,1,0:T(8,128)(4,1)}, pred[4,128,16]{2,1,0:T(8,128)(4,1)S(1)}, u32[]{:S(2)}) copy-start(pred[4,128,16]{2,1,0:T(8,128)(4,1)S(1)} %copy.61) | copy-start | bytes 24580
  225.3 37.6 %copy-start.27 = (f32[128]{0:T(128)}, f32[128]{0:T(128)S(1)}, u32[]{:S(2)}) copy-start(f32[128]{0:T(128)S(1)} %add_rsqrt_fusion.1) | copy-start | bytes 1540
  318.3 367.7 %reduce-scatter.3.cloned.1.call-start = ((), (), s32[]{:S(2)}) async-start(), calls=%async_computation.4 | async-start | bytes 28311552 | tf_op jit(solution)/shard_map/reduce_scatter | solution.py:1523
  421.4 54.5 %all-to-all-start.1 = ((bf16[4,128,2048]{2,1,0:T(8,128)(2,1)}), bf16[4,128,2048]{2,1,0:T(8,128)(2,1)S(1)}, u32[]{:S(2)}, u32[]{:S(2)}) async-start(bf16[4,128,2048]{2,1,0:T(8,128)(2,1)} %bitcast.152), calls=%async_computation.1 | async-start | bytes 4194304 | tf_op jit(solution)/shard_map/all_to_all | solution.py:1537
  427.1 3.8 copy-start.28
  430.1 2.5 copy-start.9
  433.7 32.8 %copy-start.23 = (bf16[128,16]{1,0:T(8,128)(2,1)S(1)}, bf16[128,16]{1,0:T(8,128)(2,1)}, u32[]{:S(2)}) copy-start(bf16[128,16]{1,0:T(8,128)(2,1)} %copy-done.22) | copy-start | bytes 12292
  464.2 75.3 %collective-permute-start.2 = (bf16[2048,384]{1,0:T(8,128)(2,1)}, bf16[2048,384]{1,0:T(8,128)(2,1)}, u32[]{:S(2)}, u32[]{:S(2)}) collective-permute-start(bf16[2048,384]{1,0:T(8,128)(2,1)} %bitcast.123), channel_id=1, source_target_pairs={{0,2},{2,0},{1,3},{3,1},{4,6},{6,4},{5,7},{7,5},{8,10},{10,8},{9,1... | collective-permute-start | bytes 4718600 | tf_op jit(solution)/shard_map/ppermute | solution.py:1552
  467.8 4.8 copy-start.16
  471.0 2.7 copy-start.6
  525.8 11.8 %copy-start.5 = (bf16[4,128,2048]{2,1,0:T(8,128)(2,1)S(1)}, bf16[4,128,2048]{2,1,0:T(8,128)(2,1)}, u32[]{:S(2)}) copy-start(bf16[4,128,2048]{2,1,0:T(8,128)(2,1)} %copy-done.4) | copy-start | bytes 6291460
  568.3 9.2 %copy-start.25 = (f32[1,2048]{1,0:T(1,128)S(1)}, f32[1,2048]{1,0:T(1,128)}, u32[]{:S(2)}) copy-start(f32[1,2048]{1,0:T(1,128)} %reshape.381.gain_ref) | copy-start | bytes 24580
  577.5 4.2 copy-start.33
  577.5 4.2 copy-start.34
  580.4 88.3 %collective-permute-start.3 = (bf16[64,2048]{1,0:T(8,128)(2,1)S(1)}, bf16[64,2048]{1,0:T(8,128)(2,1)}, u32[]{:S(2)}, u32[]{:S(2)}) collective-permute-start(bf16[64,2048]{1,0:T(8,128)(2,1)S(1)} %reduce_sum.121), channel_id=1, source_target_pairs={{0,0},{1,8},{2,16},{3,24},{4,1},{5,9},{6,17},{7,25},{8,2},{9,10},{... | collective-permute-start | bytes 786440 | tf_op jit(solution)/shard_map/ppermute | solution.py:1590
  584.7 73.6 %copy-start.1 = (bf16[4,128,2048]{2,1,0:T(8,128)(2,1)S(1)}, bf16[4,128,2048]{2,1,0:T(8,128)(2,1)}, u32[]{:S(2)}) copy-start(bf16[4,128,2048]{2,1,0:T(8,128)(2,1)} %copy-done) | copy-start | bytes 6291460
  658.3 2.7 copy-start.8
  658.3 2.7 copy-start.32
  658.4 3.0 copy-start.13
  (16 other events, 24.7 us)
Sparse Core Ops, SparseCore 0:
  12.5 169.0 all-gather.6
  184.1 127.0 all-gather.4
  318.4 185.5 reduce-scatter.4
  507.5 178.4 reduce-scatter.2
